TPU v7x, 512 devices: a whole 4x8x8 slice. The times are simulated.
512 devices in a mesh: dp: 16 (over y, core), seq: 32 (over x, z).
Axes of the slice: x: 4, y: 8, z: 8, core: 2. Of those that a mesh axis runs over, the one named last changes fastest.
Arguments:
- frame_in: bfloat16 [16, 4608, 1024], P('dp', 'seq'), may hold values from -120 to 120
- token_ids: int32 [16, 32, 60], P('dp', 'seq'), may hold values from 0 to 3327
- durations: int32 [16, 32, 60], P('dp', 'seq'), may hold values from 1 to 4, 144 in all within a row
- valid_len: int32 [16], P('dp'), may hold values from 1152 to 4608, as said below
- t_bin: int32 [16], P('dp'), may hold values from 0 to 63
- token_table: bfloat16 [3328, 512], P('seq'), may hold values from -6 to 6
- enc_weight: bfloat16 [512, 1024], replicated, may hold values from -0.25 to 0.25
- mod_table: float32 [64, 2048], replicated, may hold values from -1.2 to 2.5
- w_query: bfloat16 [1024, 512], P('seq'), may hold values from -0.1875 to 0.1875
- w_key: bfloat16 [1024, 512], P('seq'), may hold values from -0.1875 to 0.1875
- w_value: bfloat16 [1024, 512], P('seq'), may hold values from -0.1875 to 0.1875
- attn_grad: bfloat16 [16, 4608, 512], P('dp', 'seq'), may hold values from -6 to 6
Outputs:
- attn_out: bfloat16 [16, 4608, 512], P('dp', 'seq')
- frame_grad: bfloat16 [16, 4608, 1024], P('dp', 'seq')
- query_weight_grad: float32 [1024, 512], P('seq')
- key_weight_grad: float32 [1024, 512], P('seq')
- value_weight_grad: float32 [1024, 512], P('seq')
Inputs may be any that keep to these rules, and one draw needn't show every extreme that they name: In every slab the 60 durations sum to 144, so each token's frames lie in its own slab; some token lasts 4 frames. `valid_len`: some recording is valid over all 4608 frames.
All inputs are finite; a program needn't handle non-finite values.
Results may differ from a plain program's by a relative error of at most 0.017.
The roundings to bfloat16 on the way count: a program that leaves them out, or rounds other values in their place, can miss the bound.
Values may be sent and summed in bfloat16 or wider, within the bound.
A program may use at most 64 MiB of HBM per device.

v0:
```python
import math

import jax
import jax.numpy as jnp
from jax import lax
from jax.sharding import PartitionSpec as P

D = 1024
HEADS = 8
HD = 64
BLK = 48
QW = 512


def extended_2(cells, sides, width):
    for axis, dim in sides:
        count = lax.axis_size(axis)
        ends = count - 1
        head = lax.slice_in_dim(cells, 0, width, axis=dim)
        tail = lax.slice_in_dim(cells, cells.shape[dim] - width, cells.shape[dim], axis=dim)
        cells = jnp.concatenate(
            [
                lax.ppermute(tail, axis, [(i, (i + 1) % count) for i in range(ends)]),
                cells,
                lax.ppermute(head, axis, [((i + 1) % count, i) for i in range(ends)]),
            ],
            axis=dim,
        )
    return cells


def shifted(block, axis, distance):
    devices = range(lax.axis_size(axis))
    route = [(i - distance, i) for i in devices if i - distance in devices]
    return lax.ppermute(block, axis, route)


def attend_window(
    q_blocks, key_ext, value_ext, grad_out, query_pos, key_pos, valid_end, frames_total
):
    n_blocks = q_blocks.shape[0]
    block_len = q_blocks.shape[1]
    key_win = jnp.concatenate([key_ext[offset : offset + n_blocks] for offset in range(4)], axis=1)
    value_win = jnp.concatenate(
        [value_ext[offset : offset + n_blocks] for offset in range(4)], axis=1
    )
    key_here = key_pos[:, None, :]
    allowed = (
        (key_here >= 0)
        & (key_here < frames_total)
        & ((key_here < valid_end) | (query_pos[:, :, None] >= valid_end))
    )
    row_mask = allowed[:, None]
    inv_scale = 1.0 / math.sqrt(q_blocks.shape[-1])
    scores = (
        jnp.einsum("bqhd,bkhd->bhqk", q_blocks, key_win, preferred_element_type=jnp.float32)
        * inv_scale
    )
    scores = jnp.where(row_mask, scores, -1e30)
    row_top = jnp.max(scores, axis=-1, keepdims=True)
    shifted_exp = jnp.where(row_mask, jnp.exp(scores - row_top), 0.0)
    attn_prob = shifted_exp / jnp.sum(shifted_exp, axis=-1, keepdims=True)
    probs_low = attn_prob.astype(jnp.bfloat16)
    mixed_out = jnp.einsum(
        "bhqk,bkhd->bqhd", probs_low, value_win, preferred_element_type=jnp.float32
    ).astype(jnp.bfloat16)
    grad_probs = jnp.einsum(
        "bqhd,bkhd->bhqk", grad_out, value_win, preferred_element_type=jnp.float32
    )
    centre = jnp.sum(attn_prob * grad_probs, axis=-1, keepdims=True)
    grad_scores = (attn_prob * (grad_probs - centre) * inv_scale).astype(jnp.bfloat16)
    grad_query = jnp.einsum(
        "bhqk,bkhd->bqhd", grad_scores, key_win, preferred_element_type=jnp.float32
    ).astype(jnp.bfloat16)
    key_terms = jnp.einsum(
        "bhqk,bqhd->bkhd", grad_scores, q_blocks, preferred_element_type=jnp.float32
    )
    value_terms = jnp.einsum(
        "bhqk,bqhd->bkhd", probs_low, grad_out, preferred_element_type=jnp.float32
    )
    win_terms = jnp.concatenate([key_terms, value_terms], axis=2)
    pieces = win_terms.reshape(n_blocks, 4, block_len, win_terms.shape[2], win_terms.shape[3])
    folded = jnp.zeros((n_blocks + 3,) + pieces.shape[2:], jnp.float32)
    for offset in range(4):
        folded = folded + jnp.pad(pieces[:, offset], ((offset, 3 - offset), (0, 0), (0, 0), (0, 0)))
    return (mixed_out, grad_query, folded)


def pick_rows(wanted, table_piece):
    inside = (wanted >= 0) & (wanted < table_piece.shape[0])
    picked = jnp.take(table_piece, jnp.clip(wanted, 0, table_piece.shape[0] - 1), axis=0)
    return jnp.where(inside[:, None], picked, jnp.zeros_like(picked))


def shards(
    frame_in,
    token_ids,
    durations,
    valid_len,
    t_bin,
    token_table,
    enc_weight,
    mod_table,
    w_query,
    w_key,
    w_value,
    attn_grad,
):
    frames = frame_in[0]
    n_frames = frames.shape[0]
    seq_count = lax.axis_size("seq")
    seq_index = lax.axis_index("seq")
    dp_count = lax.axis_size("dp")
    frames_total = n_frames * seq_count
    valid_end = valid_len[0]
    wanted = token_ids[0, 0]
    token_emb = pick_rows(wanted, lax.all_gather(token_table, "seq", axis=0, tiled=True))
    token_ends = jnp.cumsum(durations[0, 0])
    local_pos = jnp.arange(n_frames, dtype=jnp.int32)
    owner_tok = jnp.sum((token_ends[None, :] <= local_pos[:, None]).astype(jnp.int32), axis=1)
    frame_emb = jnp.take(token_emb, owner_tok, axis=0)
    hidden_in = frames.astype(jnp.float32) + jnp.dot(
        frame_emb, enc_weight, preferred_element_type=jnp.float32
    )
    root_ms = jnp.sqrt(jnp.mean(hidden_in * hidden_in, axis=1, keepdims=True) + 1e-06)
    normed = hidden_in / root_ms
    modulation = lax.dynamic_index_in_dim(mod_table, t_bin[0], 0, keepdims=False)
    gain_part = 1.0 + modulation[:D]
    shift_part = modulation[D:]
    modulated = (normed * gain_part + shift_part).astype(jnp.bfloat16)
    shard_cat = jnp.concatenate([w_query, w_key, w_value], axis=1)
    weights_all = lax.all_gather(shard_cat, "seq", axis=0, tiled=True)
    projected = jnp.dot(modulated, weights_all, preferred_element_type=jnp.float32).astype(
        jnp.bfloat16
    )
    queries = projected[:, :QW]
    keys_values = projected[:, QW:]
    padded = extended_2(keys_values, (("seq", 0),), 2 * BLK)
    extended = padded[: n_frames + 3 * BLK]
    n_blocks = n_frames // BLK
    ext_blocks = extended.reshape(n_blocks + 3, BLK, 2, HEADS, HD)
    global_pos = seq_index * n_frames + local_pos
    query_pos = global_pos.reshape(n_blocks, BLK)
    key_pos = (
        seq_index * n_frames
        + (jnp.arange(n_blocks, dtype=jnp.int32)[:, None] - 2) * BLK
        + jnp.arange(4 * BLK, dtype=jnp.int32)[None, :]
    )
    live_rows = global_pos < valid_end
    grad_live = jnp.where(live_rows[:, None], attn_grad[0], jnp.zeros_like(attn_grad[0]))
    attn_blocks, query_grad, ext_grad = attend_window(
        queries.reshape(n_blocks, BLK, HEADS, HD),
        ext_blocks[:, :, 0],
        ext_blocks[:, :, 1],
        grad_live.reshape(n_blocks, BLK, HEADS, HD),
        query_pos,
        key_pos,
        valid_end,
        frames_total,
    )
    ext_rows = ext_grad.reshape(n_frames + 3 * BLK, 2 * QW)
    from_next = shifted(ext_rows[: 2 * BLK], "seq", -1)
    from_prev = shifted(ext_rows[n_frames + 2 * BLK :], "seq", 1)
    own_rows = ext_rows[2 * BLK : 2 * BLK + n_frames]
    own_rows = (
        own_rows
        + jnp.pad(from_next, ((n_frames - 2 * BLK, 0), (0, 0)))
        + jnp.pad(from_prev, ((0, n_frames - BLK), (0, 0)))
    )
    grad_cat = jnp.concatenate(
        [query_grad.reshape(n_frames, QW), own_rows.astype(jnp.bfloat16)], axis=1
    )
    grad_scale = 1.0 / math.sqrt(dp_count * frames_total)
    per_seq = lax.psum_scatter(
        (
            lax.dot_general(
                modulated, grad_cat, (((0,), (0,)), ((), ())), preferred_element_type=jnp.float32
            )
            * grad_scale
        ).astype(jnp.bfloat16),
        "seq",
        scatter_dimension=0,
        tiled=True,
    ).astype(jnp.float32)
    weight_grad = lax.psum(per_seq, "dp")
    hidden_grad = lax.dot_general(
        grad_cat, weights_all, (((1,), (1,)), ((), ())), preferred_element_type=jnp.float32
    )
    scaled_grad = hidden_grad * gain_part
    frame_grad = (
        scaled_grad - normed * jnp.mean(scaled_grad * normed, axis=1, keepdims=True)
    ) / root_ms
    return (
        attn_blocks.reshape(n_frames, QW)[None],
        frame_grad.astype(jnp.bfloat16)[None],
        weight_grad[:, :QW],
        weight_grad[:, QW : 2 * QW],
        weight_grad[:, 2 * QW :],
    )


def solution(mesh):
    placed = (
        P("dp", "seq", None),
        P("dp", "seq", None),
        P("dp", "seq", None),
        P("dp"),
        P("dp"),
        P("seq", None),
        P(),
        P(),
        P("seq", None),
        P("seq", None),
        P("seq", None),
        P("dp", "seq", None),
    )
    return jax.shard_map(
        shards,
        mesh=mesh,
        in_specs=placed,
        out_specs=(
            P("dp", "seq", None),
            P("dp", "seq", None),
            P("seq", None),
            P("seq", None),
            P("seq", None),
        ),
        check_vma=False,
    )
```

profile of v0, /device:TPU:1, one launch (start us, length us, event | category | flops | bytes accessed | tf_op | source)
XLA Modules:
  0.0 551.8 jit_solution(4595249403937196069)
XLA Ops:
  7.2 0.7 all-gather.3.cloned.1.call-update
  8.0 1.4 pad_maximum_fusion.8
  10.8 0.8 copy.50
  11.6 0.1 reduce
  11.8 1.9 squeeze.30
  13.7 0.7 fusion.38
  14.5 0.9 dynamic-slice_add_fusion
  15.3 0.7 compare_and_fusion
  16.0 0.7 and_bitcast_fusion
  16.7 82.8 %all-gather.3.cloned.1.call-done = bf16[3328,512]{1,0:T(8,128)(2,1)} async-done(((bf16[104,512]{1,0:T(8,128)(2,1)}), bf16[3328,512]{1,0:T(8,128)(2,1)}) %all-gather.3.cloned.1.call-update) | async-done | bytes 3407888 | tf_op jit(solution)/shard_map/all_gather | solution.py:117
  99.6 3.1 gather_fusion
  102.8 0.9 gather_fusion.1
  103.7 0.5 multiply_reduce_fusion.2
  104.2 81.1 %all-gather.5.cloned.1.call-done = bf16[1024,1536]{1,0:T(8,128)(2,1)} async-done(((bf16[32,1536]{1,0:T(8,128)(2,1)}), bf16[1024,1536]{1,0:T(8,128)(2,1)}) %all-gather.5.cloned.1.call-update) | async-done | bytes 3145744 | tf_op jit(solution)/shard_map/all_gather | solution.py:132
  185.3 2.6 convolution_convert_fusion
  187.9 2.8 collective-permute-start
  190.8 1.5 collective-permute-start.1
  192.4 0.9 reshape.221
  193.4 3.8 collective-permute-done.1
  197.2 0.7 reshape.220
  198.0 1.5 fusion.53
  199.4 1.3 copy.72
  200.7 2.1 copy.74
  202.8 1.0 copy.73
  203.8 1.0 copy.71
  204.7 1.0 copy.70
  205.7 0.3 copy.69
  206.0 1.0 copy.68
  207.0 0.3 copy.75
  207.3 3.3 fusion.56
  210.6 2.1 convolution_bitcast_fusion
  212.7 2.0 fusion.24
  214.7 10.4 %convolution_bitcast_fusion.1 = f32[3,192,8,64]{1,3,2,0:T(8,128)} fusion(f32[3,8,48,192]{3,2,1,0:T(8,128)} %fusion.24, bf16[3,48,8,64]{3,2,1,0:T(8,128)(2,1)} %reshape.221, f32[3,8,48,192]{3,2,1,0:T(8,128)} %get-tuple-element.29, f32[3,8,48]{2,1,0:T(8,128)S(1)} %get-tuple-element.28), kind=kOutput, calls=%fused_computation.10 | convolution fusion | flops 29861184 | bytes 3101184 | tf_op jit(solution)/shard_map/bhqk,bqhd->bkhd/dot_general | solution.py:75
  225.1 3.5 pad_maximum_fusion
  228.6 5.9 %copy.64 = f32[3,192,16,64]{3,2,1,0:T(8,128)} copy(f32[3,192,16,64]{1,3,2,0:T(8,128)} %pad_maximum_fusion) | data formatting | bytes 4718592 | tf_op jit(solution)/shard_map/concatenate | solution.py:81
  234.5 2.7 slice_bitcast_fusion.3
  237.2 0.3 pad_add_fusion
  237.6 0.7 copy-done.1
  238.2 0.4 copy-done.3
  238.7 1.4 copy-done.5
  240.1 1.0 slice.179
  241.1 2.2 slice.152
  243.2 1.4 collective-permute-start.2
  244.7 0.2 copy-done.4
  244.9 0.8 pad_add_fusion.1
  245.7 1.8 slice.154
  247.5 4.5 collective-permute-start.3
  252.0 10.3 %fusion.11 = bf16[3,48,8,64]{3,1,2,0:T(8,128)(2,1)S(1)} fusion(f32[3,8,48,192]{3,2,1,0:T(8,128)} %fusion.24, bf16[3,48,8,64]{1,3,2,0:T(8,128)(2,1)} %bitcast.85, bf16[3,48,8,64]{1,3,2,0:T(8,128)(2,1)} %bitcast.80, bf16[3,48,8,64]{1,3,2,0:T(8,128)(2,1)} %bitcast.83, bf16[3,48,8,64]{1,3,2,0:T(8,128)(2,1)} %bitcast.79, ...), kind=kOutput, calls=%fused_computation.28 | convolution fusion | flops 32294208 | bytes 2511360 | tf_op jit(solution)/shard_map/bhqk,bkhd->bqhd/dot_general | solution.py:72
  262.3 0.2 reshape.222
  262.6 0.3 slice.150
  263.0 1.2 add_convert_fusion
  264.2 0.7 copy-done.23
  264.9 2.7 multiply_convert_fusion
  267.7 0.9 copy-done.11
  268.6 0.1 copy-done.13
  268.7 0.1 copy-done.15
  268.8 0.1 copy-done.17
  269.0 2.2 fusion.10
  271.2 0.9 broadcast_in_dim_reshape.4
  272.1 3.3 multiply_reduce_fusion.1
  275.4 0.9 fusion.21
  276.3 218.2 %reduce-scatter.2.cloned.1.call-done = bf16[32,1536]{1,0:T(8,128)(2,1)} async-done(((bf16[1024,1536]{1,0:T(8,128)(2,1)}), bf16[32,1536]{1,0:T(8,128)(2,1)}) %reduce-scatter.2.cloned.1.call-update) | async-done | bytes 98320 | tf_op jit(solution)/shard_map/reduce_scatter | solution.py:174
  494.5 50.1 %all-reduce.7 = f32[32,1536]{1,0:T(8,128)S(1)} all-reduce(bf16[32,1536]{1,0:T(8,128)(2,1)} %reduce-scatter.2.cloned.1.call-done), channel_id=1, replica_groups=mesh['dp'=16,'seq'=32] {'dp'}, use_global_device_ids=true, to_apply=%region_8.9 | all-reduce | flops 49152 | bytes 294912 | tf_op jit(solution)/shard_map/psum | solution.py:185
  544.6 0.7 fusion.55
  (90 shorter events, 1.1 us)
Async XLA Ops:
  7.2 96.5 %copy-start = (bf16[512,1024]{1,0:T(8,128)(2,1)S(1)}, bf16[512,1024]{1,0:T(8,128)(2,1)}, u32[]{:S(2)}) copy-start(bf16[512,1024]{1,0:T(8,128)(2,1)} %param.18) | copy-start | bytes 3145732
  7.2 92.4 %all-gather.3.cloned.1.call-start = ((), (), s32[]{:S(2)}) async-start(), calls=%async_computation.1 | async-start | bytes 3514368 | tf_op jit(solution)/shard_map/all_gather | solution.py:117
  7.9 177.4 %all-gather.5.cloned.1.call-start = ((), (), s32[]{:S(2)}) async-start(), calls=%async_computation.2 | async-start | bytes 3244032 | tf_op jit(solution)/shard_map/all_gather | solution.py:132
  9.4 485.1 %reduce-scatter.2.cloned.1.call-start = ((), (), s32[]{:S(2)}) async-start(), calls=%async_computation.3 | async-start | bytes 3244032 | tf_op jit(solution)/shard_map/reduce_scatter | solution.py:174
  11.7 91.9 %copy-start.22 = (bf16[1,144,1024]{2,1,0:T(8,128)(2,1)S(1)}, bf16[1,144,1024]{2,1,0:T(8,128)(2,1)}, u32[]{:S(2)}) copy-start(bf16[1,144,1024]{2,1,0:T(8,128)(2,1)} %param.12) | copy-start | bytes 884740
  15.3 170.0 %copy-start.24 = (f32[1,1024]{1,0:T(1,128)}, f32[1,1024]{1,0:T(1,128)S(1)}, u32[]{:S(2)}) copy-start(f32[1,1024]{1,0:T(1,128)S(1)} %get-tuple-element.17) | copy-start | bytes 12292
  15.3 170.0 %copy-start.27 = (f32[1,1024]{1,0:T(1,128)}, f32[1,1024]{1,0:T(1,128)S(1)}, u32[]{:S(2)}) copy-start(f32[1,1024]{1,0:T(1,128)S(1)} %get-tuple-element.18) | copy-start | bytes 12292
  104.2 83.7 %copy-start.6 = (f32[144,1024]{1,0:T(8,128)}, f32[144,1024]{1,0:T(8,128)S(1)}, u32[]{:S(2)}) copy-start(f32[144,1024]{1,0:T(8,128)S(1)} %get-tuple-element.27) | copy-start | bytes 1769476
  104.2 81.1 %copy-start.29 = (f32[144]{0:T(256)}, f32[144]{0:T(256)S(1)}, u32[]{:S(2)}) copy-start(f32[144]{0:T(256)S(1)} %add_sqrt_fusion) | copy-start | bytes 1732
  187.9 5.4 collective-permute-start
  190.8 6.4 %collective-permute-start.1 = (bf16[96,1024]{1,0:T(8,128)(2,1)S(1)}, bf16[96,1024]{1,0:T(8,128)(2,1)S(1)}, u32[]{:S(2)}, u32[]{:S(2)}) collective-permute-start(bf16[96,1024]{1,0:T(8,128)(2,1)S(1)} %get-tuple-element.20), channel_id=1, source_target_pairs={{1,0},{2,1},{3,2},{4,3},{5,4},{6,5},{7,6},{8,7},{9,8},{10,9},{11,1... | collective-permute-start | bytes 589832 | tf_op jit(solution)/shard_map/ppermute | solution.py:25
  199.4 3.3 copy-start.9
  199.4 4.3 copy-start.8
  200.7 6.6 %copy-start.18 = (bf16[3,48,1,8,64]{1,4,3,0,2:T(8,128)(2,1)}, bf16[3,48,1,8,64]{1,4,3,0,2:T(8,128)(2,1)S(1)}, u32[]{:S(2)}) copy-start(bf16[3,48,1,8,64]{1,4,3,0,2:T(8,128)(2,1)S(1)} %copy.72) | copy-start | bytes 442372
  205.7 1.6 copy-start.19
  206.0 6.7 %copy-start.14 = (bf16[3,48,1,8,64]{1,4,3,0,2:T(8,128)(2,1)}, bf16[3,48,1,8,64]{1,4,3,0,2:T(8,128)(2,1)S(1)}, u32[]{:S(2)}) copy-start(bf16[3,48,1,8,64]{1,4,3,0,2:T(8,128)(2,1)S(1)} %copy.69) | copy-start | bytes 442372
  207.3 3.3 copy-start.20
  210.6 4.1 copy-start.32
  210.6 2.1 copy-start.10
  210.6 2.1 copy-start.12
  210.6 2.1 copy-start.16
  210.6 2.1 copy-start.21
  237.2 1.0 copy-start.1
  237.2 1.4 copy-start.3
  238.7 1.4 copy-start.5
  243.2 1.4 copy-start.2
  243.2 1.6 copy-start.4
  243.2 19.7 %collective-permute-start.2 = (f32[96,1024]{1,0:T(8,128)}, f32[96,1024]{1,0:T(8,128)}, u32[]{:S(2)}, u32[]{:S(2)}) collective-permute-start(f32[96,1024]{1,0:T(8,128)} %slice.152), channel_id=1, source_target_pairs={{1,0},{2,1},{3,2},{4,3},{5,4},{6,5},{7,6},{8,7},{9,8},{10,9},{11,1... | collective-permute-start | bytes 1179656 | tf_op jit(solution)/shard_map/ppermute | solution.py:35
  244.9 7.1 %copy-start.33 = (f32[3,8,48]{2,1,0:T(8,128)S(1)}, f32[3,8,48]{2,1,0:T(8,128)}, u32[]{:S(2)}) copy-start(f32[3,8,48]{2,1,0:T(8,128)} %copy-done.32) | copy-start | bytes 13828
  247.5 15.5 %collective-permute-start.3 = (f32[48,1024]{1,0:T(8,128)}, f32[48,1024]{1,0:T(8,128)}, u32[]{:S(2)}, u32[]{:S(2)}) collective-permute-start(f32[48,1024]{1,0:T(8,128)} %slice.154), channel_id=1, source_target_pairs={{0,1},{1,2},{2,3},{3,4},{4,5},{5,6},{6,7},{7,8},{8,9},{9,10},{10,1... | collective-permute-start | bytes 589832 | tf_op jit(solution)/shard_map/ppermute | solution.py:35
  252.0 10.6 %slice-start = ((f32[6,48,16,64]{3,2,1,0:T(8,128)}), f32[3,48,16,64]{3,2,1,0:T(8,128)S(1)}, s32[]{:S(2)}) async-start(f32[6,48,16,64]{3,2,1,0:T(8,128)} %copy-done.5), calls=%async_computation.4 | async-start | bytes 2359296 | tf_op jit(solution)/shard_map/slice | solution.py:164
  262.6 2.3 copy-start.7
  262.9 1.9 copy-start.25
  262.9 1.9 copy-start.28
  262.9 1.9 copy-start.30
  264.1 0.7 copy-start.23
  267.6 1.0 copy-start.11
  267.6 1.1 copy-start.13
  267.6 1.2 copy-start.15
  267.6 1.3 copy-start.17
  267.6 1.3 copy-start.34
  269.0 3.2 copy-start.26
  269.0 3.2 copy-start.31
Sparse Core Ops, SparseCore 0:
  11.2 88.3 all-gather.2
  103.3 81.9 all-gather.4
  267.8 226.6 reduce-scatter.1
where the time goes:
time: 555 us; the launch traced here: 552 us
  waiting for transfers between devices  387 us (70%)
  blocking collectives  50.1 us (9%)
  matrix products  39.3 us (7%)
  local copies, waits for them, and re-layouts  38.3 us (7%)
  between operations  15.5 us (3%)
  other arithmetic  11.6 us (2%)
  starting transfers between devices  10.3 us (2%)
    reduce_scatter x1, waiting for transfers between devices, shards(): lax.psum_scatter((lax.dot_general(modulated, grad_cat, (((0,), (0,)), (()...  218 us
    all_gather x1, waiting for transfers between devices, shards(): lax.all_gather(token_table, 'seq', axis=0, tiled=True)  82.8 us
    all_gather x1, waiting for transfers between devices, shards(): weights_all = lax.all_gather(shard_cat, 'seq', axis=0, tiled=True)  81.1 us
    psum x1, blocking collectives, shards(): weight_grad = lax.psum(per_seq, 'dp')  50.1 us
    unnamed x78, local copies, waits for them, and re-layouts  12.7 us
  transfers between devices with their start and end apart: 7, of which 4 were waited for; matrix products, arithmetic and copies ran while one was open for 6% of the time, Pallas kernels for 0%

commit v1 on v0

v1 whole, which is shorter than its diff:
```python
import math

import jax
import jax.numpy as jnp
from jax import lax
from jax.experimental import pallas as pl
from jax.experimental.pallas import tpu as pltpu
from jax.sharding import PartitionSpec as P

D = 1024
QW = 512
BLK = 48
NF = 144
NX = 4
NY = 8
NZ = 8
N_SEQ = NX * NZ
PIECE = 112
HALF = 256
WC = 3 * HALF
RC = WC // 2
MESH = pl.DeviceIdType.MESH
F32 = jnp.float32
BF16 = jnp.bfloat16
VMEM_LIMIT = 56 * 1024 * 1024


class Place:
    def __init__(self):
        self.dp = lax.axis_index("dp")
        self.seq = lax.axis_index("seq")
        self.c = lax.rem(self.dp, 2)
        self.y = self.dp // 2
        self.x = self.seq // NZ
        self.z = lax.rem(self.seq, NZ)
        self.sign = 1 - 2 * self.c

    def xs(self, o):
        return lax.rem(self.x + o * self.sign + NX, NX)

    def zs(self, o):
        return lax.rem(self.z + o * self.sign + NZ, NZ)

    def x_dev(self, o):
        return (self.dp, self.xs(o) * NZ + self.z)

    def z_dev(self, o):
        return (self.dp, self.x * NZ + self.zs(o))

    def seq_dev(self, o):
        return (self.dp, lax.rem(self.seq + o + N_SEQ, N_SEQ))

    def sib(self):
        return (self.dp + self.sign, self.seq)

    def y_dev(self, d):
        return (lax.rem(self.y + d, NY) * 2 + self.c, self.seq)


def enter(devices):
    barrier = pltpu.get_barrier_semaphore()
    for dev in devices:
        pl.semaphore_signal(barrier, inc=1, device_id=dev, device_id_type=MESH)
    pl.semaphore_wait(barrier, len(devices))


def nn(a, b):
    return jnp.dot(a, b, preferred_element_type=F32)


def nt(a, b):
    return lax.dot_general(a, b, (((1,), (1,)), ((), ())), preferred_element_type=F32)


def tn(a, b):
    return lax.dot_general(a, b, (((0,), (0,)), ((), ())), preferred_element_type=F32)


def half_of(c, refs):
    cut = [[r[:, h * HALF : (h + 1) * HALF] for r in refs] for h in range(2)]
    low = cut[0][0] if len(refs) == 1 else jnp.concatenate(cut[0], axis=1)
    high = cut[1][0] if len(refs) == 1 else jnp.concatenate(cut[1], axis=1)
    return jnp.where(c == 0, low, high)


OFFS = (0, -1, 1, -2, 2, -3, 3, -4)


def project_kernel(
    t_bin,
    frame,
    ids,
    dur,
    table,
    wq,
    wk,
    wv,
    enc,
    mod,
    q_o,
    kv_o,
    mod_o,
    nrm_o,
    root_o,
    gain_o,
    w_o,
    tbuf,
    ssem,
    rsem,
):
    me = Place()
    c = me.c
    tbuf[c, me.x, me.z] = half_of(c, [table])
    w_o[c, me.x, me.z] = half_of(c, [wq, wk, wv])
    enter(
        [
            me.sib(),
            me.x_dev(1),
            me.x_dev(-1),
            me.z_dev(1),
            me.z_dev(-1),
            me.seq_dev(1),
            me.seq_dev(-1),
        ]
    )
    started = []

    def rc(i, src, dst, dev):
        cp = pltpu.make_async_remote_copy(
            src_ref=src,
            dst_ref=dst,
            send_sem=ssem.at[i],
            recv_sem=rsem.at[i],
            device_id=dev,
            device_id_type=MESH,
        )
        cp.start()
        started.append(cp)
        return cp

    def same(i, ref, dev):
        return rc(i, ref, ref, dev)

    def t_at(xo, zo):
        return tbuf.at[c, me.xs(xo), me.zs(zo)]

    def w_at(zo):
        return w_o.at[c, :, me.zs(zo)]

    t_zr, t_zl, t_xr, t_xl, t_xf = {}, {}, {}, {}, {}
    w_zr, w_zl = {}, {}
    w_sib, t_sib = [], {}

    def t_x_send(j):
        t_xr[j] = same(7 + j, t_at(0, OFFS[j]), me.x_dev(1))
        t_xl[j] = same(15 + j, t_at(0, OFFS[j]), me.x_dev(-1))

    def t_forward(j):
        t_xr[j].wait_recv()
        t_xf[j] = same(23 + j, t_at(-1, OFFS[j]), me.x_dev(1))

    def t_z_step(k):
        t_zr[k].wait_recv()
        if k < 4:
            t_zr[k + 1] = same(k, t_at(0, -k), me.z_dev(1))
            t_zl[k].wait_recv()
            if k < 3:
                t_zl[k + 1] = same(4 + k, t_at(0, k), me.z_dev(-1))
        t_x_send(2 * k - 1)
        if k < 4:
            t_x_send(2 * k)

    def w_sibling(zo):
        i = 45 + len(w_sib)
        w_sib.append(same(i, w_at(zo), me.sib()))

    def w_z_step(k):
        w_zr[k].wait_recv()
        if k < 4:
            w_zr[k + 1] = same(34 + k, w_at(-k), me.z_dev(1))
        w_sibling(-k)
        if k < 4:
            w_zl[k].wait_recv()
            if k < 3:
                w_zl[k + 1] = same(38 + k, w_at(k), me.z_dev(-1))
            w_sibling(k)

    def t_sibling(n, xo):
        t_sib[xo] = same(41 + n, tbuf.at[c, me.xs(xo)], me.sib())

    t_zr[1] = same(0, t_at(0, 0), me.z_dev(1))
    t_zl[1] = same(4, t_at(0, 0), me.z_dev(-1))
    w_own = w_o.at[c, me.x, me.z]
    w_xr = same(31, w_own, me.x_dev(1))
    w_xl = same(32, w_own, me.x_dev(-1))
    t_x_send(0)

    lane = lax.broadcasted_iota(jnp.int32, (64, 60), 1)
    row = lax.broadcasted_iota(jnp.int32, (64, 60), 0)
    ids_f = ids[...].astype(F32)
    ids_f = ids_f + 8.0 * jnp.floor((ids_f + 0.5) * (1.0 / 104.0))
    id_col = jnp.sum(jnp.where(lane == row, ids_f, 0.0), axis=1, keepdims=True)
    end_col = jnp.sum(
        jnp.where(lane <= row, dur[...].astype(F32), 0.0), axis=1, keepdims=True
    )
    frame_pos = lax.broadcasted_iota(jnp.int32, (64, NF), 1).astype(F32)
    tok_pos = lax.broadcasted_iota(jnp.int32, (64, NF), 0).astype(F32)
    owner = jnp.sum(jnp.where(end_col <= frame_pos, 1.0, 0.0), axis=0, keepdims=True)
    spread = jnp.where(tok_pos == owner, 1.0, 0.0).astype(BF16)
    vocab_pos = lax.broadcasted_iota(jnp.int32, (64, NZ * PIECE), 1).astype(F32)

    def emb_part(half, xo):
        base = (me.xs(xo) * (NZ * PIECE)).astype(F32)
        hot = jnp.where(id_col - base == vocab_pos, 1.0, 0.0).astype(BF16)
        return nn(hot, tbuf[half, me.xs(xo)].reshape(NZ * PIECE, HALF))

    w_xr.wait_recv()
    w_xf = same(33, w_o.at[c, me.xs(-1), me.z], me.x_dev(1))
    t_z_step(1)
    w_xl.wait_recv()
    w_xf.wait_recv()
    w_zr[1] = same(34, w_at(0), me.z_dev(1))
    w_zl[1] = same(38, w_at(0), me.z_dev(-1))
    w_sibling(0)
    t_z_step(2)
    t_forward(0)
    t_z_step(3)
    t_forward(1)
    t_forward(2)
    t_z_step(4)
    t_sibling(0, 0)
    w_z_step(1)
    for j in range(3, 8):
        t_forward(j)
    t_sibling(1, -1)
    w_z_step(2)
    own = emb_part(c, 0)
    own += emb_part(c, -1)
    for j in range(8):
        t_xl[j].wait_recv()
    t_sibling(2, 1)
    own += emb_part(c, 1)
    w_z_step(3)
    for j in range(8):
        t_xf[j].wait_recv()
    t_sibling(3, -2)
    own += emb_part(c, -2)
    t_sib[0].wait_recv()
    other = emb_part(1 - c, 0)
    t_sib[-1].wait_recv()
    t_sib[1].wait_recv()
    t_sib[-2].wait_recv()
    other += emb_part(1 - c, -1)
    other += emb_part(1 - c, 1)
    other += emb_part(1 - c, -2)
    own = own.astype(BF16)
    other = other.astype(BF16)
    tok_emb = jnp.where(
        c == 0,
        jnp.concatenate([own, other], axis=1),
        jnp.concatenate([other, own], axis=1),
    )
    frame_emb = tn(spread, tok_emb).astype(BF16)
    hidden = frame[...].astype(F32) + nn(frame_emb, enc[...])
    root = jnp.sqrt(jnp.mean(hidden * hidden, axis=1, keepdims=True) + 1e-06)
    normed = hidden / root
    picked = mod[pl.ds(t_bin[0], 1), :]
    gain = 1.0 + picked[:, :D]
    modulated = (normed * gain + picked[:, D:]).astype(BF16)
    mod_o[...] = modulated
    nrm_o[...] = normed
    root_o[...] = jnp.broadcast_to(root, root_o.shape)
    gain_o[...] = gain
    w_z_step(4)
    for cp in w_sib:
        cp.wait_recv()
    for h in range(2):
        got = nn(modulated, w_o[h].reshape(D, WC)).astype(BF16)
        lo, hi = h * HALF, (h + 1) * HALF
        q_o[:, lo:hi] = got[:, :HALF]
        kv_o[2 * BLK : 2 * BLK + NF, lo:hi] = got[:, HALF : 2 * HALF]
        kv_o[2 * BLK : 2 * BLK + NF, QW + lo : QW + hi] = got[:, 2 * HALF :]
    to_next = rc(
        53, kv_o.at[3 * BLK : 5 * BLK], kv_o.at[0 : 2 * BLK], me.seq_dev(1)
    )
    to_prev = rc(
        54, kv_o.at[2 * BLK : 3 * BLK], kv_o.at[5 * BLK : 6 * BLK], me.seq_dev(-1)
    )
    to_next.wait_recv()
    to_prev.wait_recv()
    for cp in started:
        cp.wait_send()


def attend_kernel(valid, q, kv, grad, out_o, dq_o, own_o, hp_o, hn_o, ext):
    start = lax.axis_index("seq") * NF
    valid_end = valid[0]
    ext[...] = jnp.zeros_like(ext)
    head = lax.broadcasted_iota(jnp.int32, (BLK, HALF), 1) // 64
    q_off = lax.broadcasted_iota(jnp.int32, (BLK, 4 * BLK), 0)
    k_off = lax.broadcasted_iota(jnp.int32, (BLK, 4 * BLK), 1)
    row = lax.broadcasted_iota(jnp.int32, (BLK, HALF), 0)

    def stacked(block):
        zero = jnp.zeros_like(block)
        return jnp.concatenate(
            [jnp.where(head == i, block, zero) for i in range(4)], axis=0
        ).astype(BF16)

    def merged(rows):
        total = jnp.where(head == 0, rows[:BLK], 0.0)
        for i in range(1, 4):
            total = total + jnp.where(head == i, rows[i * BLK : (i + 1) * BLK], 0.0)
        return total.astype(BF16)

    for b in range(3):
        q_pos = start + b * BLK + q_off
        k_pos = start + (b - 2) * BLK + k_off
        allowed = (k_pos >= 0) & (k_pos < N_SEQ * NF)
        allowed &= (k_pos < valid_end) | (q_pos >= valid_end)
        bias = jnp.where(allowed, 0.0, -1e30)
        bias = jnp.concatenate([bias] * 4, axis=0)
        live = (start + b * BLK + row) < valid_end
        mine = slice(b * BLK, (b + 1) * BLK)
        window = slice(b * BLK, (b + 4) * BLK)
        for h in range(2):
            lo, hi = h * HALF, (h + 1) * HALF
            q_rows = stacked(q[mine, lo:hi].astype(F32))
            g_rows = stacked(jnp.where(live, grad[mine, lo:hi].astype(F32), 0.0))
            keys = kv[window, lo:hi]
            values = kv[window, QW + lo : QW + hi]
            scores = nt(q_rows, keys) * 0.125 + bias
            top = jnp.max(scores, axis=1, keepdims=True)
            e = jnp.where(bias < 0.0, 0.0, jnp.exp(scores - top))
            prob = e / jnp.sum(e, axis=1, keepdims=True)
            low = prob.astype(BF16)
            out_o[mine, lo:hi] = merged(nn(low, values))
            g_prob = nt(g_rows, values)
            centre = jnp.sum(prob * g_prob, axis=1, keepdims=True)
            g_score = (prob * (g_prob - centre) * 0.125).astype(BF16)
            dq_o[mine, lo:hi] = merged(nn(g_score, keys))
            ext[window, lo:hi] += tn(g_score, q_rows)
            ext[window, QW + lo : QW + hi] += tn(low, g_rows)
    hp_o[...] = ext[: 2 * BLK].astype(BF16)
    own_o[...] = ext[2 * BLK : 5 * BLK]
    hn_o[...] = ext[5 * BLK :].astype(BF16)


def reduce_kernel(
    modulated,
    dq,
    own,
    hp,
    hn,
    w,
    normed,
    root,
    gain,
    fg_o,
    gq_o,
    gk_o,
    gv_o,
    from_next,
    from_prev,
    mod_sib,
    g_send,
    g_sib,
    pa,
    pb,
    azr,
    azl,
    qa,
    axr,
    axl,
    bxr,
    bxl,
    qb,
    bzr,
    bzl,
    part,
    yb,
    fin,
    ssem,
    rsem,
):
    me = Place()
    c = me.c
    enter(
        [
            me.sib(),
            me.x_dev(1),
            me.x_dev(-1),
            me.z_dev(1),
            me.z_dev(-1),
            me.seq_dev(1),
            me.seq_dev(-1),
        ]
        + [me.y_dev(d) for d in range(1, NY)]
    )
    started = []

    def rc(i, src, dst, dev):
        cp = pltpu.make_async_remote_copy(
            src_ref=src,
            dst_ref=dst,
            send_sem=ssem.at[i],
            recv_sem=rsem.at[i],
            device_id=dev,
            device_id_type=MESH,
        )
        cp.start()
        started.append(cp)
        return cp

    halo_p = rc(0, hp, from_next, me.seq_dev(-1))
    halo_n = rc(1, hn, from_prev, me.seq_dev(1))
    mod_cp = rc(2, modulated, mod_sib, me.sib())
    halo_p.wait_recv()
    halo_n.wait_recv()
    dkv = jnp.concatenate(
        [
            own[:BLK] + from_prev[...].astype(F32),
            own[BLK:] + from_next[...].astype(F32),
        ],
        axis=0,
    ).astype(BF16)
    dq_v = dq[...]
    halves = [
        jnp.concatenate(
            [
                dq_v[:, h * HALF : (h + 1) * HALF],
                dkv[:, h * HALF : (h + 1) * HALF],
                dkv[:, QW + h * HALF : QW + (h + 1) * HALF],
            ],
            axis=1,
        )
        for h in range(2)
    ]
    g_send[...] = jnp.where(c == 0, halves[1], halves[0])
    g_cp = rc(3, g_send, g_sib, me.sib())
    g_own = jnp.where(c == 0, halves[0], halves[1])
    scale = 1.0 / math.sqrt(16 * 4608)
    mod_cp.wait_recv()
    g_cp.wait_recv()
    for xi in range(NX):
        cols = slice(xi * HALF, (xi + 1) * HALF)
        term = tn(modulated[:, cols], g_own) + tn(mod_sib[:, cols], g_sib[...])
        term = (term * scale).astype(BF16)
        pa[xi] = term[:, :RC].reshape(NZ, 32, RC)
        pb[xi] = term[:, RC:].reshape(NZ, 32, RC)

    a_zr = {1: rc(4, pa.at[:, me.zs(4)], azr.at[0], me.z_dev(1))}
    a_zl = {1: rc(8, pa.at[:, me.zs(-3)], azl.at[0], me.z_dev(-1))}
    b_xr = {1: rc(14, pb.at[me.xs(2)], bxr.at[0], me.x_dev(1))}
    b_xl = rc(16, pb.at[me.xs(-1)], bxl, me.x_dev(-1))

    hidden_grad = nt(halves[0], w[0].reshape(D, WC)) + nt(
        halves[1], w[1].reshape(D, WC)
    )
    scaled = hidden_grad * gain[...]
    nrm = normed[...]
    fg_o[...] = (
        (scaled - nrm * jnp.mean(scaled * nrm, axis=1, keepdims=True)) / root[:, :1]
    ).astype(BF16)

    def add(ref, mine):
        return ref.astype(F32) + mine.astype(F32)

    def a_step(k):
        a_zr[k].wait_recv()
        if k < 4:
            azr[k - 1] = add(azr[k - 1], pa[:, me.zs(4 - k)]).astype(BF16)
            a_zr[k + 1] = rc(4 + k, azr.at[k - 1], azr.at[k], me.z_dev(1))
            a_zl[k].wait_recv()
        if k < 3:
            azl[k - 1] = add(azl[k - 1], pa[:, me.zs(k - 3)]).astype(BF16)
            a_zl[k + 1] = rc(8 + k, azl.at[k - 1], azl.at[k], me.z_dev(-1))

    a_step(1)
    b_xr[1].wait_recv()
    bxr[0] = add(bxr[0], pb[me.xs(1)]).astype(BF16)
    b_xr[2] = rc(15, bxr.at[0], bxr.at[1], me.x_dev(1))
    a_step(2)
    a_step(3)
    b_xl.wait_recv()
    b_xr[2].wait_recv()
    qb[...] = (add(pb[me.x], bxr[1]) + bxl[...].astype(F32)).astype(BF16)
    b_zr = {1: rc(17, qb.at[me.zs(4)], bzr.at[0], me.z_dev(1))}
    b_zl = {1: rc(21, qb.at[me.zs(-3)], bzl.at[0], me.z_dev(-1))}
    a_step(4)
    qa[...] = (add(pa[:, me.z], azr[3]) + azl[2].astype(F32)).astype(BF16)
    a_xr = {1: rc(11, qa.at[me.xs(2)], axr.at[0], me.x_dev(1))}
    a_xl = rc(13, qa.at[me.xs(-1)], axl, me.x_dev(-1))

    def b_step(k):
        b_zr[k].wait_recv()
        if k < 4:
            bzr[k - 1] = add(bzr[k - 1], qb[me.zs(4 - k)]).astype(BF16)
            b_zr[k + 1] = rc(17 + k, bzr.at[k - 1], bzr.at[k], me.z_dev(1))
            b_zl[k].wait_recv()
        if k < 3:
            bzl[k - 1] = add(bzl[k - 1], qb[me.zs(k - 3)]).astype(BF16)
            b_zl[k + 1] = rc(21 + k, bzl.at[k - 1], bzl.at[k], me.z_dev(-1))

    b_step(1)
    a_xr[1].wait_recv()
    axr[0] = add(axr[0], qa[me.xs(1)]).astype(BF16)
    a_xr[2] = rc(12, axr.at[0], axr.at[1], me.x_dev(1))
    b_step(2)
    b_step(3)
    a_xl.wait_recv()
    a_xr[2].wait_recv()
    sum_a = add(qa[me.x], axr[1]) + axl[...].astype(F32)
    b_step(4)
    sum_b = add(qb[me.z], bzr[3]) + bzl[2].astype(F32)
    for rt in range(4):
        part[2 * rt] = sum_a[8 * rt : 8 * rt + 8]
        part[2 * rt + 1] = sum_b[8 * rt : 8 * rt + 8]

    cps = []
    for d in range(1, NY):
        cps.append(
            rc(24 + d, part.at[lax.rem(me.y + d, NY)], yb.at[d - 1], me.y_dev(d))
        )
    total = part[me.y]
    for d in range(1, NY):
        cps[d - 1].wait_recv()
        total = total + yb[d - 1]
    fin[c, me.y] = total
    cps = []
    for d in range(1, NY):
        cps.append(rc(32 + d, fin.at[c, me.y], fin.at[c, me.y], me.y_dev(d)))
    for cp in cps:
        cp.wait_recv()
    last = rc(40, fin.at[c], fin.at[c], me.sib())
    last.wait_recv()
    for h in range(2):
        lo, hi = h * HALF, (h + 1) * HALF
        for rt in range(4):
            rows = slice(8 * rt, 8 * rt + 8)
            a, b = fin[h, 2 * rt], fin[h, 2 * rt + 1]
            gq_o[rows, lo:hi] = a[:, :HALF]
            gk_o[rows, lo:hi] = jnp.concatenate([a[:, HALF:], b[:, : RC - HALF]], axis=1)
            gv_o[rows, lo:hi] = b[:, RC - HALF :]
    for cp in started:
        cp.wait_send()


def shape(dims, kind):
    return jax.ShapeDtypeStruct(dims, kind)


def shards(
    frame_in,
    token_ids,
    durations,
    valid_len,
    t_bin,
    token_table,
    enc_weight,
    mod_table,
    w_query,
    w_key,
    w_value,
    attn_grad,
):
    vm = pl.BlockSpec(memory_space=pltpu.VMEM)
    sm = pl.BlockSpec(memory_space=pltpu.SMEM)
    table = jnp.pad(token_table, ((0, PIECE - token_table.shape[0]), (0, 0)))
    queries, keys_values, modulated, normed, root, gain, weights = pl.pallas_call(
        project_kernel,
        name="project",
        out_shape=(
            shape((NF, QW), BF16),
            shape((6 * BLK, 2 * QW), BF16),
            shape((NF, D), BF16),
            shape((NF, D), F32),
            shape((NF, 128), F32),
            shape((1, D), F32),
            shape((2, NX, NZ, 32, WC), BF16),
        ),
        in_specs=[sm] + [vm] * 9,
        out_specs=(vm,) * 7,
        scratch_shapes=[
            pltpu.VMEM((2, NX, NZ, PIECE, HALF), BF16),
            pltpu.SemaphoreType.DMA((55,)),
            pltpu.SemaphoreType.DMA((55,)),
        ],
        compiler_params=pltpu.CompilerParams(
            collective_id=0, has_side_effects=True, vmem_limit_bytes=VMEM_LIMIT
        ),
    )(
        t_bin,
        frame_in[0],
        token_ids[0],
        durations[0],
        table,
        w_query,
        w_key,
        w_value,
        enc_weight,
        mod_table,
    )
    attn_out, dq, own, hp, hn = pl.pallas_call(
        attend_kernel,
        name="attend",
        out_shape=(
            shape((NF, QW), BF16),
            shape((NF, QW), BF16),
            shape((NF, 2 * QW), F32),
            shape((2 * BLK, 2 * QW), BF16),
            shape((BLK, 2 * QW), BF16),
        ),
        in_specs=[sm] + [vm] * 3,
        out_specs=(vm,) * 5,
        scratch_shapes=[pltpu.VMEM((6 * BLK, 2 * QW), F32)],
        compiler_params=pltpu.CompilerParams(vmem_limit_bytes=VMEM_LIMIT),
    )(valid_len, queries, keys_values, attn_grad[0])
    frame_grad, gq, gk, gv = pl.pallas_call(
        reduce_kernel,
        name="reduce",
        out_shape=(
            shape((NF, D), BF16),
            shape((32, QW), F32),
            shape((32, QW), F32),
            shape((32, QW), F32),
        ),
        in_specs=[vm] * 9,
        out_specs=(vm,) * 4,
        scratch_shapes=[
            pltpu.VMEM((2 * BLK, 2 * QW), BF16),
            pltpu.VMEM((BLK, 2 * QW), BF16),
            pltpu.VMEM((NF, D), BF16),
            pltpu.VMEM((NF, WC), BF16),
            pltpu.VMEM((NF, WC), BF16),
            pltpu.VMEM((NX, NZ, 32, RC), BF16),
            pltpu.VMEM((NX, NZ, 32, RC), BF16),
            pltpu.VMEM((4, NX, 32, RC), BF16),
            pltpu.VMEM((3, NX, 32, RC), BF16),
            pltpu.VMEM((NX, 32, RC), BF16),
            pltpu.VMEM((2, 32, RC), BF16),
            pltpu.VMEM((32, RC), BF16),
            pltpu.VMEM((2, NZ, 32, RC), BF16),
            pltpu.VMEM((NZ, 32, RC), BF16),
            pltpu.VMEM((NZ, 32, RC), BF16),
            pltpu.VMEM((4, 32, RC), BF16),
            pltpu.VMEM((3, 32, RC), BF16),
            pltpu.VMEM((NY, 8, RC), F32),
            pltpu.VMEM((NY - 1, 8, RC), F32),
            pltpu.VMEM((2, NY, 8, RC), F32),
            pltpu.SemaphoreType.DMA((41,)),
            pltpu.SemaphoreType.DMA((41,)),
        ],
        compiler_params=pltpu.CompilerParams(
            collective_id=1, has_side_effects=True, vmem_limit_bytes=VMEM_LIMIT
        ),
    )(modulated, dq, own, hp, hn, weights, normed, root, gain)
    return attn_out[None], frame_grad[None], gq, gk, gv


def solution(mesh):
    placed = (
        P("dp", "seq", None),
        P("dp", "seq", None),
        P("dp", "seq", None),
        P("dp"),
        P("dp"),
        P("seq", None),
        P(),
        P(),
        P("seq", None),
        P("seq", None),
        P("seq", None),
        P("dp", "seq", None),
    )
    return jax.shard_map(
        shards,
        mesh=mesh,
        in_specs=placed,
        out_specs=(
            P("dp", "seq", None),
            P("dp", "seq", None),
            P("seq", None),
            P("seq", None),
            P("seq", None),
        ),
        check_vma=False,
    )
```

time: 555 us -> 129 us (0.23)
  waiting for transfers between devices: 387 us -> 0 us
  Pallas kernels: 0 us -> 119 us
  blocking collectives: 50.1 us -> 0 us
  matrix products: 39.3 us -> 0 us
  local copies, waits for them, and re-layouts: 38.3 us -> 7.66 us
  between operations: 15.5 us -> 1.94 us
  other arithmetic: 11.6 us -> 0 us
  starting transfers between devices: 10.3 us -> 0 us
    reduce_scatter x1 -> x0, waiting for transfers between devices: 218 us -> none  [shards(): lax.psum_scatter((lax.dot_general(modulated, grad_cat, (((0,), (0,)), (()...]
    all_gather x2 -> x0, waiting for transfers between devices: 164 us -> none  [the longest x1 82.8 us: shards(): lax.all_gather(token_table, 'seq', axis=0, tiled=True)]
    pallas_call x0 -> x3, Pallas kernels: none -> 119 us  [the longest x1 57.3 us: shards(): pl.pallas_call(reduce_kernel, name='reduce', out_shape=(shape((NF, D), BF...]
    psum x1 -> x0, blocking collectives: 50.1 us -> none  [shards(): weight_grad = lax.psum(per_seq, 'dp')]
    dot_general x9 -> x0, matrix products: 36 us -> none  [the longest x1 10.4 us: attend_window(): jnp.einsum('bhqk,bqhd->bkhd', grad_scores, q_blocks, preferred_element_ty...]
    ppermute x4 -> x0, starting transfers between devices: 10.2 us -> none  [the longest x2 5.9 us: shifted(): return lax.ppermute(block, axis, route)]
    slice x11 -> x0, local copies, waits for them, and re-layouts: 7.49 us -> none  [the longest x2 3.14 us: shards(): from_next = shifted(ext_rows[:2 * BLK], 'seq', -1)]
    unnamed x78 -> x4, local copies, waits for them, and re-layouts: 12.7 us -> 6.11 us
  transfers between devices with their start and end apart: 7 -> 0, of which waited for: 4 -> 0; matrix products, arithmetic and copies ran while one was open for 6% -> 0% of each run, Pallas kernels for 0% -> 0%
where the time goes in v1:
time: 129 us; the launch traced here: 128 us
  Pallas kernels  119 us (92%)
  local copies, waits for them, and re-layouts  7.66 us (6%)
  between operations  1.94 us (2%)
    pallas_call x1, Pallas kernels, shards(): pl.pallas_call(reduce_kernel, name='reduce', out_shape=(shape((NF, D), BF...  57.3 us
    pallas_call x1, Pallas kernels, shards(): pl.pallas_call(project_kernel, name='project', out_shape=(shape((NF, QW),...  55.9 us
    unnamed x4, local copies, waits for them, and re-layouts  6.11 us
    pallas_call x1, Pallas kernels, shards(): pl.pallas_call(attend_kernel, name='attend', out_shape=(shape((NF, QW), B...  5.51 us

profile of v1, /device:TPU:1, one launch (start us, length us, event | category | flops | bytes accessed | tf_op | source)
XLA Modules:
  0.0 128.3 jit_solution(5142427465694634072)
XLA Ops:
  1.9 1.6 %pad.4.table = bf16[112,512]{1,0:T(8,128)(2,1)} pad(bf16[104,512]{1,0:T(8,128)(2,1)} %param.17, bf16[]{:T(256)} %constant.2.clone.1), padding=0_8x0_0 | pad | bytes 221186 | tf_op jit(solution)/shard_map/jit(_pad)/pad | solution.py:569
  3.5 55.9 %project.1 = (bf16[144,512]{1,0:T(8,128)(2,1)}, bf16[288,1024]{1,0:T(8,128)(2,1)}, bf16[144,1024]{1,0:T(8,128)(2,1)}, f32[144,1024]{1,0:T(8,128)}, f32[144,128]{...) custom-call(s32[1]{0:T(128)S(6)} %copy.22.t_bin, bf16[144,1024]{1,0:T(8,128)(2,1)} %bitcast.7, ...), custom_call_target="tpu_custom_call" | custom-call | tf_op jit(solution)/shard_map/project/pallas_call | solution.py:570
  59.3 5.5 %attend.1 = (bf16[144,512]{1,0:T(8,128)(2,1)}, bf16[144,512]{1,0:T(8,128)(2,1)}, f32[144,1024]{1,0:T(8,128)}, bf16[96,1024]{1,0:T(8,128)(2,1)}, bf16[48,1024]{1,0:T(8,128)(2,1)}) custom-call(s32[1]{0:T(128)S(6)} %copy.21.valid, bf16[144,512]{1,0:T(8,128)(2,1)} %get-tuple-element.21.q, bf16[288,1024]{1,0:T(8,128)(2,1)} %get-tuple-element.22.kv, ...), custom_call_target="tpu_custom_call" | custom-call | tf_op jit(solution)/shard_map/attend/pallas_call | solution.py:604
  64.9 57.3 %reduce.1 = (bf16[144,1024]{1,0:T(8,128)(2,1)}, f32[32,512]{1,0:T(8,128)}, f32[32,512]{1,0:T(8,128)}, f32[32,512]{1,0:T(8,128)}) custom-call(bf16[144,1024]{1,0:T(8,128)(2,1)} %get-tuple-element.24.modulated, bf16[144,512]{1,0:T(8,128)(2,1)} %get-tuple-element.25.dq, f32[144,1024]{1,0:T(8,128)} %get-tuple-element.26.own, ...), custom_call_target="tpu_custom_call" | custom-call | tf_op jit(solution)/shard_map/reduce/pallas_call | solution.py:619
  122.2 1.7 %copy.23 = bf16[1,144,1024]{2,1,0:T(8,128)(2,1)} copy(bf16[1,144,1024]{2,1,0:T(8,128)(2,1)} %bitcast.6) | data formatting | bytes 589824
  123.9 1.5 %copy.24 = f32[32,512]{1,0:T(8,128)} copy(f32[32,512]{1,0:T(8,128)} %get-tuple-element.44) | data formatting | bytes 131072
  125.4 1.5 %copy.25 = f32[32,512]{1,0:T(8,128)} copy(f32[32,512]{1,0:T(8,128)} %get-tuple-element.45) | data formatting | bytes 131072
  126.8 1.5 %copy.26 = f32[32,512]{1,0:T(8,128)} copy(f32[32,512]{1,0:T(8,128)} %get-tuple-element.46) | data formatting | bytes 131072

commit v2 on v0

v2 whole, which is shorter than its diff:
```python
import math

import jax
import jax.numpy as jnp
from jax import lax
from jax.experimental import pallas as pl
from jax.experimental.pallas import tpu as pltpu
from jax.sharding import PartitionSpec as P

D = 1024
QW = 512
BLK = 48
NF = 144
NX = 4
NY = 8
NZ = 8
N_SEQ = NX * NZ
PIECE = 112
HALF = 256
WC = 3 * HALF
AC = 2 * HALF
SC = WC // 2
GROUP = 4
MESH = pl.DeviceIdType.MESH
F32 = jnp.float32
BF16 = jnp.bfloat16
VMEM_LIMIT = 56 * 1024 * 1024


class Place:
    def __init__(self):
        self.dp = lax.axis_index("dp")
        self.seq = lax.axis_index("seq")
        self.c = lax.rem(self.dp, 2)
        self.y = self.dp // 2
        self.x = self.seq // NZ
        self.z = lax.rem(self.seq, NZ)
        self.sign = 1 - 2 * self.c
        self.q = lax.rem(self.dp, GROUP)

    def xs(self, o):
        return lax.rem(self.x + o * self.sign + NX, NX)

    def zs(self, o):
        return lax.rem(self.z + o * self.sign + NZ, NZ)

    def x_dev(self, o):
        return (self.dp, self.xs(o) * NZ + self.z)

    def z_dev(self, o):
        return (self.dp, self.x * NZ + self.zs(o))

    def seq_dev(self, o):
        return (self.dp, lax.rem(self.seq + o + N_SEQ, N_SEQ))

    def sib(self):
        return (self.dp + self.sign, self.seq)

    def mate(self, d):
        return lax.rem(self.q + d, GROUP)

    def mate_dev(self, d):
        return (self.dp - self.q + self.mate(d), self.seq)

    def y_dev(self, d):
        return (lax.rem(self.y + d, NY) * 2 + self.c, self.seq)

    def dp_dev(self, d):
        return (lax.rem(self.dp + d, 2 * NY), self.seq)


def nn(a, b):
    return jnp.dot(a, b, preferred_element_type=F32)


def nt(a, b):
    return lax.dot_general(a, b, (((1,), (1,)), ((), ())), preferred_element_type=F32)


def tn(a, b):
    return lax.dot_general(a, b, (((0,), (0,)), ((), ())), preferred_element_type=F32)


def add(a, b):
    return a.astype(F32) + b.astype(F32)


def pick(index, parts):
    out = parts[0]
    for i in range(1, len(parts)):
        out = jnp.where(index == i, parts[i], out)
    return out


X_OFFS = (1, -1, 2)
Z_OFFS = (1, -1, 2, -2, 3, -3, 4)


def window_kernel(
    t_bin,
    valid,
    ids,
    dur,
    table,
    wq,
    wk,
    wv,
    frame_h,
    grad_h,
    enc_h,
    mod_h,
    att_o,
    fg_o,
    fin,
    frame,
    grad,
    enc,
    mod,
    tbuf,
    wbuf,
    idb,
    esend,
    embb,
    modb,
    nrm,
    gsend,
    gradb,
    qb,
    kvb,
    dqb,
    ext,
    hps,
    hns,
    hpr,
    hnr,
    osend,
    hsend,
    hrecv,
    pa,
    pb,
    azr,
    azl,
    qa,
    axr,
    bxr,
    qvb,
    bzr,
    part,
    yb,
    lsem,
    ssem,
    rsem,
):
    me = Place()
    c = me.c
    loads = []
    for i, (a, b) in enumerate(
        ((grad_h, grad), (frame_h, frame), (enc_h, enc), (mod_h, mod))
    ):
        loads.append(pltpu.make_async_copy(a, b, lsem.at[i]))
        loads[i].start()
    quarter = pick(me.q, [table[:, i * 128 : (i + 1) * 128].astype(F32) for i in range(4)])
    tbuf[me.x, me.z] = jnp.concatenate(
        [quarter, jnp.zeros((PIECE - 104, 128), F32)], axis=0
    ).astype(BF16)
    wbuf[me.x, me.z] = jnp.concatenate(
        [pick(c, [r[:, :HALF], r[:, HALF:]]) for r in (wq, wk, wv)], axis=1
    )
    idb[me.q] = jnp.where(
        lax.broadcasted_iota(jnp.int32, (8, 128), 0) == 0,
        jnp.concatenate([ids[...].astype(F32), jnp.zeros((1, 68), F32)], axis=1),
        valid[0].astype(F32),
    )
    barrier = pltpu.get_barrier_semaphore()
    peers = [me.dp_dev(d) for d in range(1, 2 * NY)]
    peers += [me.x_dev(o) for o in X_OFFS] + [me.z_dev(o) for o in Z_OFFS]
    peers += [me.seq_dev(1), me.seq_dev(-1)]
    for dev in peers:
        pl.semaphore_signal(barrier, inc=1, device_id=dev, device_id_type=MESH)
    pl.semaphore_wait(barrier, len(peers))
    started = []

    def rc(src, dst, dev):
        i = len(started)
        cp = pltpu.make_async_remote_copy(
            src_ref=src,
            dst_ref=dst,
            send_sem=ssem.at[i],
            recv_sem=rsem.at[i],
            device_id=dev,
            device_id_type=MESH,
        )
        cp.start()
        started.append(cp)
        return cp

    def same(ref, dev):
        return rc(ref, ref, dev)

    def t_at(xo, zo):
        return tbuf.at[me.xs(xo), me.zs(zo)]

    def w_at(xo, zo):
        return wbuf.at[me.xs(xo), me.zs(zo)]

    id_cp = [same(idb.at[me.q], me.mate_dev(d)) for d in range(1, GROUP)]
    t_z = {o: same(t_at(0, 0), me.z_dev(o)) for o in Z_OFFS}
    t_x = {}

    def t_x_send(zo):
        for xo in X_OFFS:
            t_x[xo, zo] = same(t_at(0, zo), me.x_dev(xo))

    w_r, w_l = {}, {}

    def w_start(xo):
        w_r[xo, 1] = same(w_at(xo, 0), me.z_dev(1))
        w_l[xo, 1] = same(w_at(xo, 0), me.z_dev(-1))

    def w_step(xo, k):
        w_r[xo, k].wait_recv()
        if k < 4:
            w_r[xo, k + 1] = same(w_at(xo, -k), me.z_dev(1))
            w_l[xo, k].wait_recv()
        if k < 3:
            w_l[xo, k + 1] = same(w_at(xo, k), me.z_dev(-1))

    W_ROWS = (0, -1, 1, 2)
    t_x_send(0)
    w_x = {o: same(w_at(0, 0), me.x_dev(o)) for o in X_OFFS}
    w_start(0)
    loads[0].wait()
    gsend[...] = pick(c, [grad[:, HALF:], grad[:, :HALF]])
    gradb[0] = pick(c, [grad[:, :HALF], grad[:, HALF:]])
    g_cp = rc(gsend, gradb.at[1], me.sib())

    lane = lax.broadcasted_iota(jnp.int32, (64, 60), 1)
    row = lax.broadcasted_iota(jnp.int32, (64, 60), 0)
    end_col = jnp.sum(
        jnp.where(lane <= row, dur[...].astype(F32), 0.0), axis=1, keepdims=True
    )
    frame_pos = lax.broadcasted_iota(jnp.int32, (64, NF), 1).astype(F32)
    tok_pos = lax.broadcasted_iota(jnp.int32, (64, NF), 0).astype(F32)
    owner = jnp.sum(jnp.where(end_col <= frame_pos, 1.0, 0.0), axis=0, keepdims=True)
    spread = jnp.where(tok_pos == owner, 1.0, 0.0).astype(BF16)
    for cp in id_cp:
        cp.wait_recv()
    lane = lax.broadcasted_iota(jnp.int32, (64, 128), 1)
    row = lax.broadcasted_iota(jnp.int32, (64, 128), 0)
    id_cols = []
    for i in range(GROUP):
        row_ids = idb[i][:1]
        row_ids = row_ids + 8.0 * jnp.floor((row_ids + 0.5) * (1.0 / 104.0))
        id_cols.append(
            jnp.sum(jnp.where(lane == row, row_ids, 0.0), axis=1, keepdims=True)
        )
    id_col = jnp.concatenate(id_cols, axis=0)
    vocab_pos = lax.broadcasted_iota(jnp.int32, (GROUP * 64, NZ * PIECE), 1)
    vocab_pos = vocab_pos.astype(F32)

    def emb_part(xo):
        base = (me.xs(xo) * (NZ * PIECE)).astype(F32)
        hot = jnp.where(id_col - base == vocab_pos, 1.0, 0.0).astype(BF16)
        return nn(hot, tbuf[me.xs(xo)].reshape(NZ * PIECE, 128))

    for o in (1, -1):
        t_z[o].wait_recv()
        t_x_send(-o)
    for o in (1, -1, 2):
        w_x[o].wait_recv()
        w_start(-o if o != 2 else 2)
    for o in (2, -2, 3, -3, 4):
        t_z[o].wait_recv()
        t_x_send(-o if o != 4 else 4)
    emb = emb_part(0)
    for xo in W_ROWS:
        w_step(xo, 1)
    for o in (1, -1):
        for zo in (0,) + Z_OFFS:
            t_x[o, zo].wait_recv()
        emb += emb_part(-o)
    for xo in W_ROWS:
        w_step(xo, 2)
    for zo in (0,) + Z_OFFS:
        t_x[2, zo].wait_recv()
    emb += emb_part(2)
    esend[...] = emb.astype(BF16).reshape(GROUP, 64, 128)
    embb[me.q] = esend[me.q]
    e_cp = [
        rc(esend.at[me.mate(d)], embb.at[me.q], me.mate_dev(d)) for d in range(1, GROUP)
    ]
    for cp in e_cp:
        cp.wait_recv()
    tok_emb = jnp.concatenate([embb[i] for i in range(GROUP)], axis=1)
    frame_emb = tn(spread, tok_emb).astype(BF16)
    for cp in loads[1:]:
        cp.wait()
    hidden = frame[...].astype(F32) + nn(frame_emb, enc[...])
    root = jnp.sqrt(jnp.mean(hidden * hidden, axis=1, keepdims=True) + 1e-06)
    normed = hidden / root
    picked = mod[pl.ds(t_bin[0], 1), :]
    gain = 1.0 + picked[:, :D]
    nrm[...] = normed
    modb[0] = (normed * gain + picked[:, D:]).astype(BF16)
    m_cp = [
        rc(modb.at[0, i * BLK : (i + 1) * BLK], modb.at[1, i * BLK : (i + 1) * BLK], me.sib())
        for i in range(3)
    ]
    for k in (3, 4):
        for xo in W_ROWS:
            w_step(xo, k)
    weights = wbuf[...].reshape(D, WC)

    halos = {}
    for r in range(2):
        if r == 1:
            for cp in m_cp:
                cp.wait_recv()
        got = nn(modb[r], weights).astype(BF16)
        kvb[r, 2 * BLK : 5 * BLK] = got[:, HALF:]
        halos[r] = [
            rc(kvb.at[r, 3 * BLK : 5 * BLK], kvb.at[r, : 2 * BLK], me.seq_dev(1)),
            rc(kvb.at[r, 2 * BLK : 3 * BLK], kvb.at[r, 5 * BLK :], me.seq_dev(-1)),
        ]
        qb[r] = got[:, :HALF]
    g_cp.wait_recv()

    start = me.seq * NF
    head = lax.broadcasted_iota(jnp.int32, (BLK, HALF), 1) // 64
    q_off = lax.broadcasted_iota(jnp.int32, (BLK, 4 * BLK), 0)
    k_off = lax.broadcasted_iota(jnp.int32, (BLK, 4 * BLK), 1)
    live_row = lax.broadcasted_iota(jnp.int32, (BLK, HALF), 0)
    ext[...] = jnp.zeros_like(ext)

    def stacked(block):
        return jnp.concatenate(
            [jnp.where(head == i, block, 0.0) for i in range(4)], axis=0
        ).astype(BF16)

    def merged(rows):
        return pick(head, [rows[i * BLK : (i + 1) * BLK] for i in range(4)]).astype(BF16)

    back = {}
    for r in range(2):
        for cp in halos[r]:
            cp.wait_recv()
        slot = me.q if r == 0 else me.q + me.sign
        valid_end = idb[slot][1:2, 0:1]
        for b in range(3):
            q_pos = start + b * BLK + q_off
            k_pos = start + (b - 2) * BLK + k_off
            inside = (k_pos >= 0) & (k_pos < N_SEQ * NF)
            open_pair = (k_pos.astype(F32) < valid_end) | (q_pos.astype(F32) >= valid_end)
            bias = jnp.where(inside & open_pair, 0.0, -1e30)
            bias = jnp.concatenate([bias] * 4, axis=0)
            live = (start + b * BLK + live_row).astype(F32) < valid_end
            mine = slice(b * BLK, (b + 1) * BLK)
            window = slice(b * BLK, (b + 4) * BLK)
            q_rows = stacked(qb[r, mine].astype(F32))
            g_rows = stacked(jnp.where(live, gradb[r, mine].astype(F32), 0.0))
            keys = kvb[r, window, :HALF]
            values = kvb[r, window, HALF:]
            scores = nt(q_rows, keys) * 0.125 + bias
            top = jnp.max(scores, axis=1, keepdims=True)
            e = jnp.where(bias < 0.0, 0.0, jnp.exp(scores - top))
            prob = e / jnp.sum(e, axis=1, keepdims=True)
            low = prob.astype(BF16)
            mixed = merged(nn(low, values))
            if r == 0:
                att_o[c, mine] = mixed
            else:
                osend[mine] = mixed
            g_prob = nt(g_rows, values)
            centre = jnp.sum(prob * g_prob, axis=1, keepdims=True)
            g_score = (prob * (g_prob - centre) * 0.125).astype(BF16)
            dqb[r, mine] = merged(nn(g_score, keys))
            ext[r, window, :HALF] += tn(g_score, q_rows)
            ext[r, window, HALF:] += tn(low, g_rows)
            if b == 1:
                hps[r] = ext[r, : 2 * BLK].astype(BF16)
                back[r] = [rc(hps.at[r], hpr.at[r], me.seq_dev(-1))]
        hns[r] = ext[r, 5 * BLK :].astype(BF16)
        back[r].append(rc(hns.at[r], hnr.at[r], me.seq_dev(1)))
    o_cp = rc(osend, att_o.at[c], me.sib())
    grads = []
    for r in range(2):
        for cp in back[r]:
            cp.wait_recv()
        own = ext[r, 2 * BLK : 5 * BLK]
        dkv = jnp.concatenate(
            [own[:BLK] + hnr[r].astype(F32), own[BLK:] + hpr[r].astype(F32)], axis=0
        )
        grads.append(jnp.concatenate([dqb[r], dkv.astype(BF16)], axis=1))

    scale = 1.0 / math.sqrt(16 * 4608)
    b_x, a_r, a_l = {}, {}, {}
    for xo in (2, 1, -1, 0):
        xi = me.xs(xo)
        cols = pl.ds(pl.multiple_of(xi * HALF, HALF), HALF)
        term = tn(modb[0, :, cols], grads[0]) + tn(modb[1, :, cols], grads[1])
        term = (term * scale).astype(BF16)
        pa[xi] = term[:, :AC].reshape(NZ, 32, AC)
        pb[xi] = term[:, AC:].reshape(NZ, 32, HALF)
        a_r[xo, 1] = rc(pa.at[xi, me.zs(4)], azr.at[0, xi], me.z_dev(1))
        a_l[xo, 1] = rc(pa.at[xi, me.zs(-3)], azl.at[0, xi], me.z_dev(-1))
        if xo != 0:
            b_x[xo] = rc(pb.at[xi], bxr.at[X_OFFS.index(xo)], me.x_dev(xo))

    def a_step(k):
        for xo in (2, 1, -1, 0):
            xi = me.xs(xo)
            a_r[xo, k].wait_recv()
            if k < 4:
                azr[k - 1, xi] = add(azr[k - 1, xi], pa[xi, me.zs(4 - k)]).astype(BF16)
                a_r[xo, k + 1] = rc(azr.at[k - 1, xi], azr.at[k, xi], me.z_dev(1))
                a_l[xo, k].wait_recv()
            if k < 3:
                azl[k - 1, xi] = add(azl[k - 1, xi], pa[xi, me.zs(k - 3)]).astype(BF16)
                a_l[xo, k + 1] = rc(azl.at[k - 1, xi], azl.at[k, xi], me.z_dev(-1))

    hsend[...] = nt(grads[1], weights).astype(BF16)
    h_cp = rc(hsend, hrecv, me.sib())
    a_step(1)
    hidden_grad = nt(grads[0], weights)
    a_step(2)
    for cp in b_x.values():
        cp.wait_recv()
    total = pb[me.x].astype(F32)
    for i in range(3):
        total = total + bxr[i].astype(F32)
    qvb[...] = total.astype(BF16)
    b_z = [
        rc(qvb.at[me.zs(o)], bzr.at[i], me.z_dev(o)) for i, o in enumerate(Z_OFFS)
    ]
    a_step(3)
    h_cp.wait_recv()
    scaled = (hidden_grad + hrecv[...].astype(F32)) * gain
    normed = nrm[...]
    fg_o[...] = (
        (scaled - normed * jnp.mean(scaled * normed, axis=1, keepdims=True)) / root
    ).astype(BF16)
    a_step(4)
    for xo in (2, 1, -1, 0):
        xi = me.xs(xo)
        got = add(azr[3, xi], azl[2, xi]) + pa[xi, me.z].astype(F32)
        qa[xi] = got.astype(BF16)
    a_x = [rc(qa.at[me.xs(o)], axr.at[i], me.x_dev(o)) for i, o in enumerate(X_OFFS)]
    sum_b = qvb[me.z].astype(F32)
    for i, cp in enumerate(b_z):
        cp.wait_recv()
        sum_b = sum_b + bzr[i].astype(F32)
    sum_a = qa[me.x].astype(F32)
    for i, cp in enumerate(a_x):
        cp.wait_recv()
        sum_a = sum_a + axr[i].astype(F32)
    for rt in range(4):
        rows = slice(8 * rt, 8 * rt + 8)
        part[2 * rt] = sum_a[rows, :SC]
        part[2 * rt + 1] = jnp.concatenate([sum_a[rows, SC:], sum_b[rows]], axis=1)

    y_cp = [
        rc(part.at[lax.rem(me.y + d, NY)], yb.at[d - 1], me.y_dev(d))
        for d in range(1, NY)
    ]
    total = part[me.y]
    for d in range(1, NY):
        y_cp[d - 1].wait_recv()
        total = total + yb[d - 1]
    fin[c, me.y] = total
    for cp in [same(fin.at[c, me.y], me.dp_dev(d)) for d in range(1, 2 * NY)]:
        cp.wait_recv()
    o_cp.wait_recv()
    for cp in started:
        cp.wait_send()


def finish_kernel(att, fg, fin, att_o, fg_o, gq_o, gk_o, gv_o):
    fg_o[...] = fg[...]
    for h in range(2):
        lo, hi = h * HALF, (h + 1) * HALF
        att_o[:, lo:hi] = att[h]
        for rt in range(4):
            rows = slice(8 * rt, 8 * rt + 8)
            a, b = fin[h, 2 * rt], fin[h, 2 * rt + 1]
            gq_o[rows, lo:hi] = a[:, :HALF]
            gk_o[rows, lo:hi] = jnp.concatenate([a[:, HALF:], b[:, : SC - HALF]], axis=1)
            gv_o[rows, lo:hi] = b[:, SC - HALF :]


def shape(dims, kind):
    return jax.ShapeDtypeStruct(dims, kind)


def shards(
    frame_in,
    token_ids,
    durations,
    valid_len,
    t_bin,
    token_table,
    enc_weight,
    mod_table,
    w_query,
    w_key,
    w_value,
    attn_grad,
):
    vm = pl.BlockSpec(memory_space=pltpu.VMEM)
    sm = pl.BlockSpec(memory_space=pltpu.SMEM)
    hb = pl.BlockSpec(memory_space=pl.ANY)
    att, fg, fin = pl.pallas_call(
        window_kernel,
        name="window",
        out_shape=(
            shape((2, NF, HALF), BF16),
            shape((NF, D), BF16),
            shape((2, NY, 8, SC), F32),
        ),
        in_specs=[sm] * 2 + [vm] * 6 + [hb] * 4,
        out_specs=(vm,) * 3,
        scratch_shapes=[
            pltpu.VMEM((NF, D), BF16),
            pltpu.VMEM((NF, QW), BF16),
            pltpu.VMEM((QW, D), BF16),
            pltpu.VMEM((64, 2 * D), F32),
            pltpu.VMEM((NX, NZ, PIECE, 128), BF16),
            pltpu.VMEM((NX, NZ, 32, WC), BF16),
            pltpu.VMEM((GROUP, 8, 128), F32),
            pltpu.VMEM((GROUP, 64, 128), BF16),
            pltpu.VMEM((GROUP, 64, 128), BF16),
            pltpu.VMEM((2, NF, D), BF16),
            pltpu.VMEM((NF, D), F32),
            pltpu.VMEM((NF, HALF), BF16),
            pltpu.VMEM((2, NF, HALF), BF16),
            pltpu.VMEM((2, NF, HALF), BF16),
            pltpu.VMEM((2, 6 * BLK, 2 * HALF), BF16),
            pltpu.VMEM((2, NF, HALF), BF16),
            pltpu.VMEM((2, 6 * BLK, 2 * HALF), F32),
            pltpu.VMEM((2, 2 * BLK, 2 * HALF), BF16),
            pltpu.VMEM((2, BLK, 2 * HALF), BF16),
            pltpu.VMEM((2, 2 * BLK, 2 * HALF), BF16),
            pltpu.VMEM((2, BLK, 2 * HALF), BF16),
            pltpu.VMEM((NF, HALF), BF16),
            pltpu.VMEM((NF, D), BF16),
            pltpu.VMEM((NF, D), BF16),
            pltpu.VMEM((NX, NZ, 32, AC), BF16),
            pltpu.VMEM((NX, NZ, 32, HALF), BF16),
            pltpu.VMEM((4, NX, 32, AC), BF16),
            pltpu.VMEM((3, NX, 32, AC), BF16),
            pltpu.VMEM((NX, 32, AC), BF16),
            pltpu.VMEM((3, 32, AC), BF16),
            pltpu.VMEM((3, NZ, 32, HALF), BF16),
            pltpu.VMEM((NZ, 32, HALF), BF16),
            pltpu.VMEM((7, 32, HALF), BF16),
            pltpu.VMEM((NY, 8, SC), F32),
            pltpu.VMEM((NY - 1, 8, SC), F32),
            pltpu.SemaphoreType.DMA((4,)),
            pltpu.SemaphoreType.DMA((170,)),
            pltpu.SemaphoreType.DMA((170,)),
        ],
        compiler_params=pltpu.CompilerParams(
            collective_id=0, has_side_effects=True, vmem_limit_bytes=VMEM_LIMIT
        ),
    )(
        t_bin,
        valid_len,
        token_ids[0],
        durations[0],
        token_table,
        w_query,
        w_key,
        w_value,
        frame_in[0],
        attn_grad[0],
        enc_weight,
        mod_table,
    )
    att, fg, gq, gk, gv = pl.pallas_call(
        finish_kernel,
        name="finish",
        out_shape=(
            shape((NF, QW), BF16),
            shape((NF, D), BF16),
            shape((32, QW), F32),
            shape((32, QW), F32),
            shape((32, QW), F32),
        ),
        in_specs=[vm] * 3,
        out_specs=(vm,) * 5,
    )(att, fg, fin)
    return att[None], fg[None], gq, gk, gv


def solution(mesh):
    placed = (
        P("dp", "seq", None),
        P("dp", "seq", None),
        P("dp", "seq", None),
        P("dp"),
        P("dp"),
        P("seq", None),
        P(),
        P(),
        P("seq", None),
        P("seq", None),
        P("seq", None),
        P("dp", "seq", None),
    )
    return jax.shard_map(
        shards,
        mesh=mesh,
        in_specs=placed,
        out_specs=(
            P("dp", "seq", None),
            P("dp", "seq", None),
            P("seq", None),
            P("seq", None),
            P("seq", None),
        ),
        check_vma=False,
    )
```

time: 555 us -> 95.5 us (0.17)
  waiting for transfers between devices: 387 us -> 0 us
  Pallas kernels: 0 us -> 93.4 us
  blocking collectives: 50.1 us -> 0 us
  matrix products: 39.3 us -> 0 us
  local copies, waits for them, and re-layouts: 38.3 us -> 0 us
  between operations: 15.5 us -> 1.93 us
  other arithmetic: 11.6 us -> 0 us
  starting transfers between devices: 10.3 us -> 0 us
    reduce_scatter x1 -> x0, waiting for transfers between devices: 218 us -> none  [shards(): lax.psum_scatter((lax.dot_general(modulated, grad_cat, (((0,), (0,)), (()...]
    all_gather x2 -> x0, waiting for transfers between devices: 164 us -> none  [the longest x1 82.8 us: shards(): lax.all_gather(token_table, 'seq', axis=0, tiled=True)]
    pallas_call x0 -> x2, Pallas kernels: none -> 93.4 us  [the longest x1 91.5 us: shards(): pl.pallas_call(window_kernel, name='window', out_shape=(shape((2, NF, HAL...]
    psum x1 -> x0, blocking collectives: 50.1 us -> none  [shards(): weight_grad = lax.psum(per_seq, 'dp')]
    dot_general x9 -> x0, matrix products: 36 us -> none  [the longest x1 10.4 us: attend_window(): jnp.einsum('bhqk,bqhd->bkhd', grad_scores, q_blocks, preferred_element_ty...]
    unnamed x78 -> x0, local copies, waits for them, and re-layouts: 12.7 us -> none
    ppermute x4 -> x0, starting transfers between devices: 10.2 us -> none  [the longest x2 5.9 us: shifted(): return lax.ppermute(block, axis, route)]
    slice x11 -> x0, local copies, waits for them, and re-layouts: 7.49 us -> none  [the longest x2 3.14 us: shards(): from_next = shifted(ext_rows[:2 * BLK], 'seq', -1)]
  transfers between devices with their start and end apart: 7 -> 0, of which waited for: 4 -> 0; matrix products, arithmetic and copies ran while one was open for 6% -> 0% of each run, Pallas kernels for 0% -> 0%
where the time goes in v2:
time: 95.5 us; the launch traced here: 95.4 us
  Pallas kernels  93.4 us (98%)
  between operations  1.93 us (2%)
    pallas_call x1, Pallas kernels, shards(): pl.pallas_call(window_kernel, name='window', out_shape=(shape((2, NF, HAL...  91.5 us
    pallas_call x1, Pallas kernels, shards(): pl.pallas_call(finish_kernel, name='finish', out_shape=(shape((NF, QW), B...  1.93 us

profile of v2, /device:TPU:1, one launch (start us, length us, event | category | flops | bytes accessed | tf_op | source)
XLA Modules:
  0.0 95.4 jit_solution(17579478010461349966)
XLA Ops:
  1.9 91.5 %window.1 = (bf16[2,144,256]{2,1,0:T(8,128)(2,1)}, bf16[144,1024]{1,0:T(8,128)(2,1)}, f32[2,8,8,384]{3,2,1,0:T(8,128)}) custom-call(s32[1]{0:T(128)S(6)} %copy.18.t_bin, s32[1]{0:T(128)S(6)} %copy.17.valid, s32[1,60]{1,0:T(1,128)} %bitcast.8, s32[1,60]{1,0:T(1,128)} %bitcast.9, bf16[104,512]{1,0:T(8,128)(2,1)} %table.1, bf16[32,512]{1,0:T(8,128)(2,1)} %wq.1, ...), custom_call_target="tpu_custom_call" | custom-call | tf_op jit(solution)/shard_map/window/pallas_call | solution.py:511
  93.4 1.9 %finish.1 = (bf16[144,512]{1,0:T(8,128)(2,1)}, bf16[144,1024]{1,0:T(8,128)(2,1)}, f32[32,512]{1,0:T(8,128)}, f32[32,512]{1,0:T(8,128)}, f32[32,512]{1,0:T(8,128)}) custom-call(bf16[2,144,256]{2,1,0:T(8,128)(2,1)} %get-tuple-element.13.att, bf16[144,1024]{1,0:T(8,128)(2,1)} %get-tuple-element.14.fg, f32[2,8,8,384]{3,2,1,0:T(8,128)} %get-tuple-element.15.fin), custom_call_target="tpu_custom_call" | custom-call | tf_op jit(solution)/shard_map/finish/pallas_call | solution.py:578

commit v3 on v2

--- a/solution.py
+++ b/solution.py
@@ -15,12 +15,12 @@
 NY = 8
 NZ = 8
 N_SEQ = NX * NZ
-PIECE = 112
+PIECE = 64
 HALF = 256
 WC = 3 * HALF
 AC = 2 * HALF
-SC = WC // 2
-GROUP = 4
+SC = WC // 4
+GROUP = 8
 MESH = pl.DeviceIdType.MESH
 F32 = jnp.float32
 BF16 = jnp.bfloat16
@@ -64,9 +64,6 @@
 
     def y_dev(self, d):
         return (lax.rem(self.y + d, NY) * 2 + self.c, self.seq)
-
-    def dp_dev(self, d):
-        return (lax.rem(self.dp + d, 2 * NY), self.seq)
 
 
 def nn(a, b):
@@ -118,6 +115,8 @@
     mod,
     tbuf,
     wbuf,
+    wmine,
+    wswap,
     idb,
     esend,
     embb,
@@ -159,20 +158,33 @@
     ):
         loads.append(pltpu.make_async_copy(a, b, lsem.at[i]))
         loads[i].start()
-    quarter = pick(me.q, [table[:, i * 128 : (i + 1) * 128].astype(F32) for i in range(4)])
-    tbuf[me.x, me.z] = jnp.concatenate(
-        [quarter, jnp.zeros((PIECE - 104, 128), F32)], axis=0
+    quarter = pick(
+        lax.rem(me.q, 4), [table[:, i * 128 : (i + 1) * 128].astype(F32) for i in range(4)]
+    )
+    upper = me.q // 4
+    odd = lax.rem(me.y, 2)
+    tbuf[me.x, me.z] = pick(
+        upper,
+        [
+            quarter[:PIECE],
+            jnp.concatenate(
+                [quarter[PIECE:], jnp.zeros((2 * PIECE - 104, 128), F32)], axis=0
+            ),
+        ],
     ).astype(BF16)
-    wbuf[me.x, me.z] = jnp.concatenate(
-        [pick(c, [r[:, :HALF], r[:, HALF:]]) for r in (wq, wk, wv)], axis=1
-    )
+    w_q, w_k, w_v = [pick(c, [r[:, :HALF], r[:, HALF:]]) for r in (wq, wk, wv)]
+    wbuf[me.x, me.z] = w_k
+    w_m = pick(odd, [w_q, w_v])
+    for i in range(2):
+        wmine[i, me.x, me.z] = w_m[:, i * 128 : (i + 1) * 128]
     idb[me.q] = jnp.where(
         lax.broadcasted_iota(jnp.int32, (8, 128), 0) == 0,
         jnp.concatenate([ids[...].astype(F32), jnp.zeros((1, 68), F32)], axis=1),
         valid[0].astype(F32),
     )
     barrier = pltpu.get_barrier_semaphore()
-    peers = [me.dp_dev(d) for d in range(1, 2 * NY)]
+    peers = [me.y_dev(d) for d in range(1, NY)]
+    peers += [me.mate_dev(d) for d in range(1, GROUP, 2)]
     peers += [me.x_dev(o) for o in X_OFFS] + [me.z_dev(o) for o in Z_OFFS]
     peers += [me.seq_dev(1), me.seq_dev(-1)]
     for dev in peers:
@@ -197,6 +209,21 @@
     def same(ref, dev):
         return rc(ref, ref, dev)
 
+    def cut(src, dst, dev, size):
+        rows = [pl.ds(i, size) for i in range(0, src.shape[0], size)]
+        return [rc(src.at[r], dst.at[r], dev) for r in rows]
+
+    drained = [0]
+
+    def drain():
+        for cp in started[drained[0] :]:
+            cp.wait_send()
+        drained[0] = len(started)
+
+    def arrive(cps):
+        for cp in cps:
+            cp.wait_recv()
+
     def t_at(xo, zo):
         return tbuf.at[me.xs(xo), me.zs(zo)]
 
@@ -225,14 +252,28 @@
         if k < 3:
             w_l[xo, k + 1] = same(w_at(xo, k), me.z_dev(-1))
 
+    w_y = []
+
+    def y_send(xo):
+        for i, d in ((0, 1), (1, NY - 1)):
+            w_y.append(
+                rc(wmine.at[i, me.xs(xo)], wswap.at[i, me.xs(xo)], me.y_dev(d))
+            )
+
     W_ROWS = (0, -1, 1, 2)
+
+    def w_steps(k):
+        for xo in W_ROWS:
+            w_step(xo, k)
+
+    w_x = {o: same(w_at(0, 0), me.x_dev(o)) for o in X_OFFS}
     t_x_send(0)
-    w_x = {o: same(w_at(0, 0), me.x_dev(o)) for o in X_OFFS}
     w_start(0)
+    wm_z = [same(wmine.at[:, me.x, me.z], me.z_dev(o)) for o in Z_OFFS]
     loads[0].wait()
     gsend[...] = pick(c, [grad[:, HALF:], grad[:, :HALF]])
     gradb[0] = pick(c, [grad[:, :HALF], grad[:, HALF:]])
-    g_cp = rc(gsend, gradb.at[1], me.sib())
+    g_cp = cut(gsend, gradb.at[1], me.sib(), 48)
 
     lane = lax.broadcasted_iota(jnp.int32, (64, 60), 1)
     row = lax.broadcasted_iota(jnp.int32, (64, 60), 0)
@@ -250,7 +291,10 @@
     id_cols = []
     for i in range(GROUP):
         row_ids = idb[i][:1]
-        row_ids = row_ids + 8.0 * jnp.floor((row_ids + 0.5) * (1.0 / 104.0))
+        owner_row = jnp.floor((row_ids + 0.5) * (1.0 / 104.0))
+        inner = row_ids - 104.0 * owner_row - (PIECE * upper).astype(F32)
+        held = (inner >= 0.0) & (inner < float(PIECE))
+        row_ids = jnp.where(held, owner_row * PIECE + inner, -1.0)
         id_cols.append(
             jnp.sum(jnp.where(lane == row, row_ids, 0.0), axis=1, keepdims=True)
         )
@@ -272,26 +316,32 @@
     for o in (2, -2, 3, -3, 4):
         t_z[o].wait_recv()
         t_x_send(-o if o != 4 else 4)
+    w_steps(1)
+    arrive(wm_z)
+    wm_x = {o: same(wmine.at[:, me.x], me.x_dev(o)) for o in X_OFFS}
+    y_send(0)
     emb = emb_part(0)
-    for xo in W_ROWS:
-        w_step(xo, 1)
-    for o in (1, -1):
+    for zo in (0,) + Z_OFFS:
+        t_x[1, zo].wait_recv()
+    w_steps(2)
+    emb += emb_part(-1)
+    for o, xo in ((-1, 1), (2, 2)):
         for zo in (0,) + Z_OFFS:
             t_x[o, zo].wait_recv()
-        emb += emb_part(-o)
-    for xo in W_ROWS:
-        w_step(xo, 2)
-    for zo in (0,) + Z_OFFS:
-        t_x[2, zo].wait_recv()
-    emb += emb_part(2)
+        emb += emb_part(xo)
     esend[...] = emb.astype(BF16).reshape(GROUP, 64, 128)
     embb[me.q] = esend[me.q]
     e_cp = [
         rc(esend.at[me.mate(d)], embb.at[me.q], me.mate_dev(d)) for d in range(1, GROUP)
     ]
-    for cp in e_cp:
-        cp.wait_recv()
-    tok_emb = jnp.concatenate([embb[i] for i in range(GROUP)], axis=1)
+    w_steps(3)
+    for o in X_OFFS:
+        wm_x[o].wait_recv()
+        y_send(-o if o != 2 else 2)
+    arrive(e_cp)
+    tok_emb = jnp.concatenate(
+        [add(embb[i], embb[i + 4]).astype(BF16) for i in range(4)], axis=1
+    )
     frame_emb = tn(spread, tok_emb).astype(BF16)
     for cp in loads[1:]:
         cp.wait()
@@ -302,28 +352,42 @@
     gain = 1.0 + picked[:, :D]
     nrm[...] = normed
     modb[0] = (normed * gain + picked[:, D:]).astype(BF16)
-    m_cp = [
-        rc(modb.at[0, i * BLK : (i + 1) * BLK], modb.at[1, i * BLK : (i + 1) * BLK], me.sib())
-        for i in range(3)
-    ]
-    for k in (3, 4):
-        for xo in W_ROWS:
-            w_step(xo, k)
-    weights = wbuf[...].reshape(D, WC)
+    m_cp = cut(modb.at[0], modb.at[1], me.sib(), 16)
+    w_steps(4)
 
     halos = {}
+
+    def send_halo(r, i):
+        halos[r] = halos.get(r, []) + [
+            rc(
+                kvb.at[i, r, 3 * BLK : 5 * BLK],
+                kvb.at[i, r, : 2 * BLK],
+                me.seq_dev(1),
+            ),
+            rc(
+                kvb.at[i, r, 2 * BLK : 3 * BLK],
+                kvb.at[i, r, 5 * BLK :],
+                me.seq_dev(-1),
+            ),
+        ]
+
+    w_key = wbuf[...].reshape(D, HALF)
     for r in range(2):
         if r == 1:
-            for cp in m_cp:
-                cp.wait_recv()
-        got = nn(modb[r], weights).astype(BF16)
-        kvb[r, 2 * BLK : 5 * BLK] = got[:, HALF:]
-        halos[r] = [
-            rc(kvb.at[r, 3 * BLK : 5 * BLK], kvb.at[r, : 2 * BLK], me.seq_dev(1)),
-            rc(kvb.at[r, 2 * BLK : 3 * BLK], kvb.at[r, 5 * BLK :], me.seq_dev(-1)),
-        ]
-        qb[r] = got[:, :HALF]
-    g_cp.wait_recv()
+            arrive(m_cp)
+        kvb[0, r, 2 * BLK : 5 * BLK] = nn(modb[r], w_key).astype(BF16)
+        send_halo(r, 0)
+    w_mine = jnp.concatenate([wmine[i].reshape(D, 128) for i in range(2)], axis=1)
+    mine_r = [nn(modb[r], w_mine) for r in range(2)]
+    arrive(w_y)
+    w_swap = jnp.concatenate([wswap[i].reshape(D, 128) for i in range(2)], axis=1)
+    for r in range(2):
+        swap_r = nn(modb[r], w_swap)
+        kvb[1, r, 2 * BLK : 5 * BLK] = pick(odd, [swap_r, mine_r[r]]).astype(BF16)
+        send_halo(r, 1)
+        qb[r] = pick(odd, [mine_r[r], swap_r]).astype(BF16)
+    drain()
+    arrive(g_cp)
 
     start = me.seq * NF
     head = lax.broadcasted_iota(jnp.int32, (BLK, HALF), 1) // 64
@@ -358,8 +422,8 @@
             window = slice(b * BLK, (b + 4) * BLK)
             q_rows = stacked(qb[r, mine].astype(F32))
             g_rows = stacked(jnp.where(live, gradb[r, mine].astype(F32), 0.0))
-            keys = kvb[r, window, :HALF]
-            values = kvb[r, window, HALF:]
+            keys = kvb[0, r, window]
+            values = kvb[1, r, window]
             scores = nt(q_rows, keys) * 0.125 + bias
             top = jnp.max(scores, axis=1, keepdims=True)
             e = jnp.where(bias < 0.0, 0.0, jnp.exp(scores - top))
@@ -378,10 +442,10 @@
             ext[r, window, HALF:] += tn(low, g_rows)
             if b == 1:
                 hps[r] = ext[r, : 2 * BLK].astype(BF16)
-                back[r] = [rc(hps.at[r], hpr.at[r], me.seq_dev(-1))]
+                back[r] = cut(hps.at[r], hpr.at[r], me.seq_dev(-1), BLK)
         hns[r] = ext[r, 5 * BLK :].astype(BF16)
         back[r].append(rc(hns.at[r], hnr.at[r], me.seq_dev(1)))
-    o_cp = rc(osend, att_o.at[c], me.sib())
+    o_cp = cut(osend, att_o.at[c], me.sib(), BLK)
     grads = []
     for r in range(2):
         for cp in back[r]:
@@ -418,10 +482,18 @@
                 azl[k - 1, xi] = add(azl[k - 1, xi], pa[xi, me.zs(k - 3)]).astype(BF16)
                 a_l[xo, k + 1] = rc(azl.at[k - 1, xi], azl.at[k, xi], me.z_dev(-1))
 
-    hsend[...] = nt(grads[1], weights).astype(BF16)
-    h_cp = rc(hsend, hrecv, me.sib())
+    def hidden_part(g):
+        g_q, g_k, g_v = g[:, :HALF], g[:, HALF : 2 * HALF], g[:, 2 * HALF :]
+        return (
+            nt(g_k, w_key)
+            + nt(pick(odd, [g_q, g_v]), w_mine)
+            + nt(pick(odd, [g_v, g_q]), w_swap)
+        )
+
+    hsend[...] = hidden_part(grads[1]).astype(BF16)
+    h_cp = cut(hsend, hrecv, me.sib(), 16)
     a_step(1)
-    hidden_grad = nt(grads[0], weights)
+    hidden_grad = hidden_part(grads[0])
     a_step(2)
     for cp in b_x.values():
         cp.wait_recv()
@@ -433,7 +505,7 @@
         rc(qvb.at[me.zs(o)], bzr.at[i], me.z_dev(o)) for i, o in enumerate(Z_OFFS)
     ]
     a_step(3)
-    h_cp.wait_recv()
+    arrive(h_cp)
     scaled = (hidden_grad + hrecv[...].astype(F32)) * gain
     normed = nrm[...]
     fg_o[...] = (
@@ -453,25 +525,30 @@
     for i, cp in enumerate(a_x):
         cp.wait_recv()
         sum_a = sum_a + axr[i].astype(F32)
-    for rt in range(4):
-        rows = slice(8 * rt, 8 * rt + 8)
-        part[2 * rt] = sum_a[rows, :SC]
-        part[2 * rt + 1] = jnp.concatenate([sum_a[rows, SC:], sum_b[rows]], axis=1)
+    whole = jnp.concatenate([sum_a, sum_b], axis=1)
+    for i in range(NY):
+        rows, cols = slice(i // 4 * 16, i // 4 * 16 + 16), slice(i % 4 * SC, (i % 4 + 1) * SC)
+        part[i] = whole[rows, cols].astype(BF16)
 
     y_cp = [
         rc(part.at[lax.rem(me.y + d, NY)], yb.at[d - 1], me.y_dev(d))
         for d in range(1, NY)
     ]
-    total = part[me.y]
+    drain()
+    total = part[me.y].astype(F32)
     for d in range(1, NY):
         y_cp[d - 1].wait_recv()
-        total = total + yb[d - 1]
-    fin[c, me.y] = total
-    for cp in [same(fin.at[c, me.y], me.dp_dev(d)) for d in range(1, 2 * NY)]:
-        cp.wait_recv()
-    o_cp.wait_recv()
-    for cp in started:
-        cp.wait_send()
+        total = total + yb[d - 1].astype(F32)
+    fin[c, me.y] = total.astype(BF16)
+    eighth = fin.at[c, me.y]
+    y_all = [same(eighth, me.y_dev(d)) for d in range(1, NY)]
+    last = [same(eighth, me.sib())]
+    for d in range(1, NY):
+        y_all[d - 1].wait_recv()
+        last.append(same(fin.at[c, lax.rem(me.y - d + NY, NY)], me.sib()))
+    arrive(last)
+    arrive(o_cp)
+    drain()
 
 
 def finish_kernel(att, fg, fin, att_o, fg_o, gq_o, gk_o, gv_o):
@@ -479,12 +556,13 @@
     for h in range(2):
         lo, hi = h * HALF, (h + 1) * HALF
         att_o[:, lo:hi] = att[h]
-        for rt in range(4):
-            rows = slice(8 * rt, 8 * rt + 8)
-            a, b = fin[h, 2 * rt], fin[h, 2 * rt + 1]
-            gq_o[rows, lo:hi] = a[:, :HALF]
-            gk_o[rows, lo:hi] = jnp.concatenate([a[:, HALF:], b[:, : SC - HALF]], axis=1)
-            gv_o[rows, lo:hi] = b[:, SC - HALF :]
+        for rt in range(2):
+            rows = slice(16 * rt, 16 * rt + 16)
+            got = [fin[h, 4 * rt + j].astype(F32) for j in range(4)]
+            got = jnp.concatenate(got, axis=1)
+            gq_o[rows, lo:hi] = got[:, :HALF]
+            gk_o[rows, lo:hi] = got[:, HALF : 2 * HALF]
+            gv_o[rows, lo:hi] = got[:, 2 * HALF :]
 
 
 def shape(dims, kind):
@@ -514,7 +592,7 @@
         out_shape=(
             shape((2, NF, HALF), BF16),
             shape((NF, D), BF16),
-            shape((2, NY, 8, SC), F32),
+            shape((2, NY, 16, SC), BF16),
         ),
         in_specs=[sm] * 2 + [vm] * 6 + [hb] * 4,
         out_specs=(vm,) * 3,
@@ -524,7 +602,9 @@
             pltpu.VMEM((QW, D), BF16),
             pltpu.VMEM((64, 2 * D), F32),
             pltpu.VMEM((NX, NZ, PIECE, 128), BF16),
-            pltpu.VMEM((NX, NZ, 32, WC), BF16),
+            pltpu.VMEM((NX, NZ, 32, HALF), BF16),
+            pltpu.VMEM((2, NX, NZ, 32, 128), BF16),
+            pltpu.VMEM((2, NX, NZ, 32, 128), BF16),
             pltpu.VMEM((GROUP, 8, 128), F32),
             pltpu.VMEM((GROUP, 64, 128), BF16),
             pltpu.VMEM((GROUP, 64, 128), BF16),
@@ -533,7 +613,7 @@
             pltpu.VMEM((NF, HALF), BF16),
             pltpu.VMEM((2, NF, HALF), BF16),
             pltpu.VMEM((2, NF, HALF), BF16),
-            pltpu.VMEM((2, 6 * BLK, 2 * HALF), BF16),
+            pltpu.VMEM((2, 2, 6 * BLK, HALF), BF16),
             pltpu.VMEM((2, NF, HALF), BF16),
             pltpu.VMEM((2, 6 * BLK, 2 * HALF), F32),
             pltpu.VMEM((2, 2 * BLK, 2 * HALF), BF16),
@@ -552,11 +632,11 @@
             pltpu.VMEM((3, NZ, 32, HALF), BF16),
             pltpu.VMEM((NZ, 32, HALF), BF16),
             pltpu.VMEM((7, 32, HALF), BF16),
-            pltpu.VMEM((NY, 8, SC), F32),
-            pltpu.VMEM((NY - 1, 8, SC), F32),
+            pltpu.VMEM((NY, 16, SC), BF16),
+            pltpu.VMEM((NY - 1, 16, SC), BF16),
             pltpu.SemaphoreType.DMA((4,)),
-            pltpu.SemaphoreType.DMA((170,)),
-            pltpu.SemaphoreType.DMA((170,)),
+            pltpu.SemaphoreType.DMA((220,)),
+            pltpu.SemaphoreType.DMA((220,)),
         ],
         compiler_params=pltpu.CompilerParams(
             collective_id=0, has_side_effects=True, vmem_limit_bytes=VMEM_LIMIT

time: 95.5 us -> 93.1 us (0.975)
  Pallas kernels: 93.4 us -> 91 us
    pallas_call x1, Pallas kernels: 91.5 us -> 89.1 us  [shards(): pl.pallas_call(window_kernel, name='window', out_shape=(shape((2, NF, HAL...]
where the time goes in v3:
time: 93.1 us; the launch traced here: 93 us
  Pallas kernels  91 us (98%)
  between operations  1.93 us (2%)
    pallas_call x1, Pallas kernels, shards(): pl.pallas_call(window_kernel, name='window', out_shape=(shape((2, NF, HAL...  89.1 us
    pallas_call x1, Pallas kernels, shards(): pl.pallas_call(finish_kernel, name='finish', out_shape=(shape((NF, QW), B...  1.91 us

profile of v3, /device:TPU:1, one launch (start us, length us, event | category | flops | bytes accessed | tf_op | source)
XLA Modules:
  0.0 93.0 jit_solution(18427572206653581434)
XLA Ops:
  1.9 89.1 %window.1 = (bf16[2,144,256]{2,1,0:T(8,128)(2,1)}, bf16[144,1024]{1,0:T(8,128)(2,1)}, bf16[2,8,16,192]{3,2,1,0:T(8,128)(2,1)}) custom-call(s32[1]{0:T(128)S(6)} %copy.18.t_bin, s32[1]{0:T(128)S(6)} %copy.17.valid, s32[1,60]{1,0:T(1,128)} %bitcast.8, s32[1,60]{1,0:T(1,128)} %bitcast.9, bf16[104,512]{1,0:T(8,128)(2,1)} %table.1, bf16[32,512]{1,0:T(8,128)(2,1)} %wq.1, ...), custom_call_target="tpu_custom_call" | custom-call | tf_op jit(solution)/shard_map/window/pallas_call | solution.py:589
  91.0 1.9 %finish.1 = (bf16[144,512]{1,0:T(8,128)(2,1)}, bf16[144,1024]{1,0:T(8,128)(2,1)}, f32[32,512]{1,0:T(8,128)}, f32[32,512]{1,0:T(8,128)}, f32[32,512]{1,0:T(8,128)}) custom-call(bf16[2,144,256]{2,1,0:T(8,128)(2,1)} %get-tuple-element.13.att, bf16[144,1024]{1,0:T(8,128)(2,1)} %get-tuple-element.14.fg, bf16[2,8,16,192]{3,2,1,0:T(8,128)(2,1)} %get-tuple-element.15.fin), custom_call_target="tpu_custom_call" | custom-call | tf_op jit(solution)/shard_map/finish/pallas_call | solution.py:658

commit v4 on v3

--- a/solution.py
+++ b/solution.py
@@ -446,41 +446,53 @@
         hns[r] = ext[r, 5 * BLK :].astype(BF16)
         back[r].append(rc(hns.at[r], hnr.at[r], me.seq_dev(1)))
     o_cp = cut(osend, att_o.at[c], me.sib(), BLK)
-    grads = []
-    for r in range(2):
-        for cp in back[r]:
-            cp.wait_recv()
-        own = ext[r, 2 * BLK : 5 * BLK]
-        dkv = jnp.concatenate(
-            [own[:BLK] + hnr[r].astype(F32), own[BLK:] + hpr[r].astype(F32)], axis=0
-        )
-        grads.append(jnp.concatenate([dqb[r], dkv.astype(BF16)], axis=1))
-
     scale = 1.0 / math.sqrt(16 * 4608)
     b_x, a_r, a_l = {}, {}, {}
-    for xo in (2, 1, -1, 0):
+    A_ROWS = (2, 1, -1, 0)
+
+    def term_of(xi, pair):
+        cols = pl.ds(pl.multiple_of(xi * HALF, HALF), HALF)
+        term = tn(modb[0, :, cols], pair[0]) + tn(modb[1, :, cols], pair[1])
+        return (term * scale).astype(BF16)
+
+    def a_start(i, xo, term):
         xi = me.xs(xo)
-        cols = pl.ds(pl.multiple_of(xi * HALF, HALF), HALF)
-        term = tn(modb[0, :, cols], grads[0]) + tn(modb[1, :, cols], grads[1])
-        term = (term * scale).astype(BF16)
-        pa[xi] = term[:, :AC].reshape(NZ, 32, AC)
-        pb[xi] = term[:, AC:].reshape(NZ, 32, HALF)
-        a_r[xo, 1] = rc(pa.at[xi, me.zs(4)], azr.at[0, xi], me.z_dev(1))
-        a_l[xo, 1] = rc(pa.at[xi, me.zs(-3)], azl.at[0, xi], me.z_dev(-1))
+        pa[i, xi] = term.reshape(NZ, 32, HALF)
+        a_r[i, xo, 1] = rc(pa.at[i, xi, me.zs(4)], azr.at[i, 0, xi], me.z_dev(1))
+        a_l[i, xo, 1] = rc(pa.at[i, xi, me.zs(-3)], azl.at[i, 0, xi], me.z_dev(-1))
+
+    def a_step(i, k):
+        for xo in A_ROWS:
+            xi = me.xs(xo)
+            a_r[i, xo, k].wait_recv()
+            if k < 4:
+                azr[i, k - 1, xi] = add(azr[i, k - 1, xi], pa[i, xi, me.zs(4 - k)]).astype(BF16)
+                a_r[i, xo, k + 1] = rc(azr.at[i, k - 1, xi], azr.at[i, k, xi], me.z_dev(1))
+                a_l[i, xo, k].wait_recv()
+            if k < 3:
+                azl[i, k - 1, xi] = add(azl[i, k - 1, xi], pa[i, xi, me.zs(k - 3)]).astype(BF16)
+                a_l[i, xo, k + 1] = rc(azl.at[i, k - 1, xi], azl.at[i, k, xi], me.z_dev(-1))
+
+    for xo in A_ROWS:
+        a_start(0, xo, term_of(me.xs(xo), [dqb[0], dqb[1]]))
+    dkv = []
+    for r in range(2):
+        arrive(back[r])
+        own = ext[r, 2 * BLK : 5 * BLK]
+        dkv.append(
+            jnp.concatenate(
+                [own[:BLK] + hnr[r].astype(F32), own[BLK:] + hpr[r].astype(F32)], axis=0
+            ).astype(BF16)
+        )
+    for xo in A_ROWS:
+        xi = me.xs(xo)
+        term = term_of(xi, dkv)
+        a_start(1, xo, term[:, :HALF])
+        pb[xi] = term[:, HALF:].reshape(NZ, 32, HALF)
         if xo != 0:
             b_x[xo] = rc(pb.at[xi], bxr.at[X_OFFS.index(xo)], me.x_dev(xo))
-
-    def a_step(k):
-        for xo in (2, 1, -1, 0):
-            xi = me.xs(xo)
-            a_r[xo, k].wait_recv()
-            if k < 4:
-                azr[k - 1, xi] = add(azr[k - 1, xi], pa[xi, me.zs(4 - k)]).astype(BF16)
-                a_r[xo, k + 1] = rc(azr.at[k - 1, xi], azr.at[k, xi], me.z_dev(1))
-                a_l[xo, k].wait_recv()
-            if k < 3:
-                azl[k - 1, xi] = add(azl[k - 1, xi], pa[xi, me.zs(k - 3)]).astype(BF16)
-                a_l[xo, k + 1] = rc(azl.at[k - 1, xi], azl.at[k, xi], me.z_dev(-1))
+    a_step(0, 1)
+    grads = [jnp.concatenate([dqb[r], dkv[r]], axis=1) for r in range(2)]
 
     def hidden_part(g):
         g_q, g_k, g_v = g[:, :HALF], g[:, HALF : 2 * HALF], g[:, 2 * HALF :]
@@ -492,9 +504,10 @@
 
     hsend[...] = hidden_part(grads[1]).astype(BF16)
     h_cp = cut(hsend, hrecv, me.sib(), 16)
-    a_step(1)
+    a_step(1, 1)
+    a_step(0, 2)
     hidden_grad = hidden_part(grads[0])
-    a_step(2)
+    a_step(1, 2)
     for cp in b_x.values():
         cp.wait_recv()
     total = pb[me.x].astype(F32)
@@ -504,18 +517,20 @@
     b_z = [
         rc(qvb.at[me.zs(o)], bzr.at[i], me.z_dev(o)) for i, o in enumerate(Z_OFFS)
     ]
-    a_step(3)
+    a_step(0, 3)
+    a_step(1, 3)
     arrive(h_cp)
     scaled = (hidden_grad + hrecv[...].astype(F32)) * gain
     normed = nrm[...]
     fg_o[...] = (
         (scaled - normed * jnp.mean(scaled * normed, axis=1, keepdims=True)) / root
     ).astype(BF16)
-    a_step(4)
-    for xo in (2, 1, -1, 0):
-        xi = me.xs(xo)
-        got = add(azr[3, xi], azl[2, xi]) + pa[xi, me.z].astype(F32)
-        qa[xi] = got.astype(BF16)
+    for i in range(2):
+        a_step(i, 4)
+        for xo in A_ROWS:
+            xi = me.xs(xo)
+            got = add(azr[i, 3, xi], azl[i, 2, xi]) + pa[i, xi, me.z].astype(F32)
+            qa[xi, :, i * HALF : (i + 1) * HALF] = got.astype(BF16)
     a_x = [rc(qa.at[me.xs(o)], axr.at[i], me.x_dev(o)) for i, o in enumerate(X_OFFS)]
     sum_b = qvb[me.z].astype(F32)
     for i, cp in enumerate(b_z):
@@ -623,10 +638,10 @@
             pltpu.VMEM((NF, HALF), BF16),
             pltpu.VMEM((NF, D), BF16),
             pltpu.VMEM((NF, D), BF16),
-            pltpu.VMEM((NX, NZ, 32, AC), BF16),
+            pltpu.VMEM((2, NX, NZ, 32, HALF), BF16),
             pltpu.VMEM((NX, NZ, 32, HALF), BF16),
-            pltpu.VMEM((4, NX, 32, AC), BF16),
-            pltpu.VMEM((3, NX, 32, AC), BF16),
+            pltpu.VMEM((2, 4, NX, 32, HALF), BF16),
+            pltpu.VMEM((2, 3, NX, 32, HALF), BF16),
             pltpu.VMEM((NX, 32, AC), BF16),
             pltpu.VMEM((3, 32, AC), BF16),
             pltpu.VMEM((3, NZ, 32, HALF), BF16),
@@ -635,8 +650,8 @@
             pltpu.VMEM((NY, 16, SC), BF16),
             pltpu.VMEM((NY - 1, 16, SC), BF16),
             pltpu.SemaphoreType.DMA((4,)),
-            pltpu.SemaphoreType.DMA((220,)),
-            pltpu.SemaphoreType.DMA((220,)),
+            pltpu.SemaphoreType.DMA((250,)),
+            pltpu.SemaphoreType.DMA((250,)),
         ],
         compiler_params=pltpu.CompilerParams(
             collective_id=0, has_side_effects=True, vmem_limit_bytes=VMEM_LIMIT

time: 93.1 us -> 92.5 us (level)
  no operation moved by 1% of the time
where the time goes in v4:
time: 92.5 us; the launch traced here: 92.3 us
  Pallas kernels  90.4 us (98%)
  between operations  1.93 us (2%)
    pallas_call x1, Pallas kernels, shards(): pl.pallas_call(window_kernel, name='window', out_shape=(shape((2, NF, HAL...  88.5 us
    pallas_call x1, Pallas kernels, shards(): pl.pallas_call(finish_kernel, name='finish', out_shape=(shape((NF, QW), B...  1.91 us

profile of v4, /device:TPU:1, one launch (start us, length us, event | category | flops | bytes accessed | tf_op | source)
XLA Modules:
  0.0 92.3 jit_solution(2371098107813506894)
XLA Ops:
  1.9 88.5 %window.1 = (bf16[2,144,256]{2,1,0:T(8,128)(2,1)}, bf16[144,1024]{1,0:T(8,128)(2,1)}, bf16[2,8,16,192]{3,2,1,0:T(8,128)(2,1)}) custom-call(s32[1]{0:T(128)S(6)} %copy.18.t_bin, s32[1]{0:T(128)S(6)} %copy.17.valid, s32[1,60]{1,0:T(1,128)} %bitcast.8, s32[1,60]{1,0:T(1,128)} %bitcast.9, bf16[104,512]{1,0:T(8,128)(2,1)} %table.1, bf16[32,512]{1,0:T(8,128)(2,1)} %wq.1, ...), custom_call_target="tpu_custom_call" | custom-call | tf_op jit(solution)/shard_map/window/pallas_call | solution.py:604
  90.4 1.9 %finish.1 = (bf16[144,512]{1,0:T(8,128)(2,1)}, bf16[144,1024]{1,0:T(8,128)(2,1)}, f32[32,512]{1,0:T(8,128)}, f32[32,512]{1,0:T(8,128)}, f32[32,512]{1,0:T(8,128)}) custom-call(bf16[2,144,256]{2,1,0:T(8,128)(2,1)} %get-tuple-element.13.att, bf16[144,1024]{1,0:T(8,128)(2,1)} %get-tuple-element.14.fg, bf16[2,8,16,192]{3,2,1,0:T(8,128)(2,1)} %get-tuple-element.15.fin), custom_call_target="tpu_custom_call" | custom-call | tf_op jit(solution)/shard_map/finish/pallas_call | solution.py:673
